TPU v7x, 32 devices: a whole 2x2x4 slice. The times are simulated.
32 devices in a mesh: sample: 16 (over z, x, core), space: 2 (over y).
Axes of the slice: x: 2, y: 2, z: 4, core: 2. Of those that a mesh axis runs over, the one named last changes fastest.
Arguments:
- volume: bfloat16 [16, 16, 16, 16, 128], P('sample', 'space'), may hold values from -6 to 6
- first_kernel: bfloat16 [3, 3, 3, 128, 128], replicated, may hold values from -0.109375 to 0.109375
- second_kernel: bfloat16 [3, 3, 3, 128, 128], replicated, may hold values from -0.109375 to 0.109375
- partner: int32 [16], replicated, may hold values from 0 to 15, as said below
- coefficient: float32 [16], replicated, may hold values from 0.25 to 0.75
- out_grad: bfloat16 [16, 16, 16, 16, 128], P('sample', 'space'), may hold values from -0.09375 to 0.09375
Outputs:
- result: bfloat16 [16, 16, 16, 16, 128], P('sample', 'space')
- first_kernel_grad: float32 [3, 3, 3, 128, 128], replicated
- second_kernel_grad: float32 [3, 3, 3, 128, 128], replicated
Inputs may be any that keep to these rules, and one draw needn't show every extreme that they name: partner[partner[i]] == i and partner[i] != i for every sample i: the samples form pairs.
All inputs are finite; a program needn't handle non-finite values.
Results may differ from a plain program's by a relative error of at most 0.013.
Values may be sent and summed in bfloat16 or wider, within the bound.
A program may use at most 64 MiB of HBM per device.

v0:
```python
import jax
import jax.numpy as jnp
from jax import lax
from jax.sharding import PartitionSpec as P


def with_halo(cells, sides, width):
    for axis, dim in sides:
        count = lax.axis_size(axis)
        ends = count - 1
        head = lax.slice_in_dim(cells, 0, width, axis=dim)
        tail = lax.slice_in_dim(cells, cells.shape[dim] - width, cells.shape[dim], axis=dim)
        cells = jnp.concatenate(
            [
                lax.ppermute(tail, axis, [(i, (i + 1) % count) for i in range(ends)]),
                cells,
                lax.ppermute(head, axis, [((i + 1) % count, i) for i in range(ends)]),
            ],
            axis=dim,
        )
    return cells


def convolve(volume_in, kernel, spread):
    return lax.conv_general_dilated(
        volume_in,
        kernel,
        (1, 1, 1),
        ((0, 0), (spread, spread), (spread, spread)),
        rhs_dilation=(spread, spread, spread),
        dimension_numbers=("NDHWC", "DHWIO", "NDHWC"),
        preferred_element_type=jnp.float32,
    )


def slope(value):
    squash = jax.nn.sigmoid(value)
    return squash * (1.0 + value * (1.0 - squash))


def kernel_grad(padded, cotangent, spread):
    sample_count, depth_size, row_size, col_size, chan_size = cotangent.shape
    framed = jnp.pad(padded, ((0, 0), (0, 0), (spread, spread), (spread, spread), (0, 0)))
    flat_cotangent = cotangent.reshape(-1, chan_size)
    plane_list = []
    for depth_tap in range(3):
        line_list = []
        for row_tap in range(3):
            tap_list = []
            for col_tap in range(3):
                window = lax.slice(
                    framed,
                    (0, depth_tap * spread, row_tap * spread, col_tap * spread, 0),
                    (
                        sample_count,
                        depth_tap * spread + depth_size,
                        row_tap * spread + row_size,
                        col_tap * spread + col_size,
                        framed.shape[4],
                    ),
                )
                tap_list.append(
                    lax.dot_general(
                        window.reshape(-1, framed.shape[4]),
                        flat_cotangent,
                        (((0,), (0,)), ((), ())),
                        preferred_element_type=jnp.float32,
                    )
                )
            line_list.append(jnp.stack(tap_list))
        plane_list.append(jnp.stack(line_list))
    return jnp.stack(plane_list)


def faces_two(tensor):
    return with_halo(tensor, (("space", 1),), 2)


def to_pieces(block):
    flat = block.reshape(block.shape[0], -1, block.shape[4])
    return lax.all_to_all(flat, "sample", split_axis=1, concat_axis=0, tiled=True)


def to_slabs(pieces, shape_out):
    return lax.all_to_all(pieces, "sample", split_axis=0, concat_axis=1, tiled=True).reshape(
        shape_out
    )


def pick(table, index):
    one_hot = (index[:, None] == jnp.arange(table.shape[0], dtype=jnp.int32)[None, :]).astype(
        jnp.float32
    )
    return jnp.dot(one_hot, table, precision=lax.Precision.HIGHEST)


def shards(volume, first_kernel, second_kernel, partner, coefficient, out_grad):
    padded_in = with_halo(volume, (("space", 1),), 1)
    pre_one = convolve(padded_in, first_kernel, 1)
    hidden = jax.nn.silu(pre_one).astype(jnp.bfloat16)
    back_share = 1.0 - pick(coefficient, partner)
    pieces = to_pieces(hidden)
    own_share = coefficient[:, None, None]
    mixed_pieces = (
        own_share * pieces + (1.0 - own_share) * jnp.take(pieces, partner, axis=0)
    ).astype(jnp.bfloat16)
    mixed = to_slabs(mixed_pieces, volume.shape)
    padded_mix = faces_two(mixed)
    pre_two = convolve(padded_mix, second_kernel, 2)
    result = jax.nn.silu(pre_two).astype(jnp.bfloat16)
    grad_two = (out_grad * slope(pre_two)).astype(jnp.bfloat16)
    second_local = kernel_grad(padded_mix, grad_two, 2)
    flipped = jnp.transpose(jnp.flip(second_kernel, (0, 1, 2)), (0, 1, 2, 4, 3))
    grad_mixed = convolve(faces_two(grad_two), flipped, 2).astype(jnp.bfloat16)
    grad_pieces = to_pieces(grad_mixed)
    grad_hidden_pieces = (
        coefficient[:, None, None] * grad_pieces
        + back_share[:, None, None] * jnp.take(grad_pieces, partner, axis=0)
    ).astype(jnp.bfloat16)
    grad_hidden = to_slabs(grad_hidden_pieces, volume.shape)
    grad_one = (grad_hidden * slope(pre_one)).astype(jnp.bfloat16)
    first_local = kernel_grad(padded_in, grad_one, 1)
    first_kernel_grad, second_kernel_grad = lax.psum(
        (first_local, second_local), ("sample", "space")
    )
    return (result, first_kernel_grad, second_kernel_grad)


def solution(mesh):
    in_specs = (
        P("sample", "space", None, None, None),
        P(),
        P(),
        P(),
        P(),
        P("sample", "space", None, None, None),
    )
    out_specs = (P("sample", "space", None, None, None), P(), P())
    return jax.shard_map(shards, mesh=mesh, in_specs=in_specs, out_specs=out_specs, check_vma=False)
```

profile of v0, /device:TPU:0, one launch (start us, length us, event | category | flops | bytes accessed | tf_op | source)
XLA Modules:
  0.0 393.3 jit_solution(17029683543450934481)
XLA Ops:
  7.2 1.0 fusion.215
  8.1 4.9 %collective-permute-start = (bf16[1,1,16,16,128]{4,3,2,1,0:T(8,128)(2,1)S(1)}, bf16[1,1,16,16,128]{4,3,2,1,0:T(8,128)(2,1)S(1)}, u32[]{:S(2)}, u32[]{:S(2)}) collective-permute-start(bf16[1,1,16,16,128]{4,3,2,1,0:T(8,128)(2,1)S(1)} %get-tuple-element.54), channel_id=1, source_target_pairs={{0,1},{2,3},{4,5},{6,7},{8,9},{10,11},{12,13},{14,15},{16,17},{18,... | collective-permute-start | bytes 196616 | tf_op jit(solution)/shard_map/ppermute | solution.py:15
  13.0 1.3 collective-permute-start.1
  14.9 0.6 copy-done.27
  15.5 1.1 constant_dynamic-update-slice_fusion.1
  16.7 2.5 collective-permute-done.1
  19.2 0.6 copy-done.29
  19.8 0.9 copy-done.11
  21.5 0.7 copy-done.35
  22.2 7.2 %add_multiply_fusion = (f32[8,16,8,3,128]{4,2,3,1,0:T(8,128)}, bf16[8,16,8,3,128]{4,2,3,1,0:T(8,128)(2,1)S(1)}) fusion(pred[8,3]{0,1:T(4,128)(4,1)S(1)} %copy-done.38, bf16[3,3,3,128,128]{4,3,2,1,0:T(8,128)(2,1)S(1)} %copy-done.35, bf16[10,16,1,7,2,128]{5,3,4,1,0,2:T(8,128)(2,1)S(1)} %slice.251, bf16[10,16,1,8,3,128]{5,3,4,1,0,2:T(8,128)(2,1)S(1)} %copy.141), kind=kOutput, calls=%fused_computation.37 | convolution fusion | flops 2613510144 | bytes 4800536 | tf_op jit(solution)/shard_map/conv_general_dilated | solution.py:25
  29.8 8.3 %copy.428 = bf16[1,2048,128]{2,0,1:T(2,128)(2,1)S(1)} copy(bf16[1,2048,128]{2,1,0:T(8,128)(2,1)S(1)} %bitcast.646) | data formatting | bytes 1048576 | tf_op jit(solution)/shard_map/reshape | solution.py:80
  38.6 11.5 %reduce = bf16[2048,128]{1,0:T(8,128)(2,1)S(1)} reduce(bf16[2048,1,128]{2,1,0:T(2,128)(2,1)S(1)} %bitcast.637, bf16[]{:T(256)} %broadcast.79), dimensions={1}, to_apply=%bitcast.629.reduce_sub_computation | reduce | bytes 1048578
  50.1 0.9 reshape.486
  51.0 5.9 %all-to-all-start = ((bf16[16,2,8192]{2,1,0:T(2,128)(2,1)}), bf16[16,2,8192]{2,1,0:T(2,128)(2,1)S(1)}, u32[]{:S(2)}, u32[]{:S(2)}) async-start(bf16[16,2,8192]{2,1,0:T(2,128)(2,1)} %reshape.486), calls=%async_computation | async-start | bytes 1048576 | tf_op jit(solution)/shard_map/all_to_all | solution.py:81
  57.0 14.4 %all-to-all-done = bf16[16,2,8192]{2,1,0:T(2,128)(2,1)S(1)} async-done(((bf16[16,2,8192]{2,1,0:T(2,128)(2,1)}), bf16[16,2,8192]{2,1,0:T(2,128)(2,1)S(1)}, u32[]{:S(2)}, u32[]{:S(2)}) %all-to-all-start) | async-done | bytes 524320 | tf_op jit(solution)/shard_map/all_to_all | solution.py:81
  72.0 0.6 gather_fusion
  73.0 18.5 %all_to_all.42 = bf16[16,128,128]{2,1,0:T(8,128)(2,1)S(1)} all-to-all(bf16[16,128,128]{2,1,0:T(8,128)(2,1)S(1)} %add_convert_fusion.1), channel_id=1, replica_groups=mesh['sample'=16,'space'=2] {'sample'}, dimensions={0} | all-to-all | bytes 1048576 | tf_op jit(solution)/shard_map/all_to_all | solution.py:85
  91.7 1.8 collective-permute-start.2
  94.2 1.3 collective-permute-start.3
  95.5 3.7 collective-permute-done.2
  99.5 1.0 constant_dynamic-update-slice_fusion.4
  100.5 3.5 collective-permute-done.3
  104.3 16.2 %fusion.14 = (bf16[1,8,16,16,128]{4,0,3,2,1:T(2,128)(2,1)S(1)}, f32[1,8,16,16,128]{4,0,3,2,1:T(1,128)}, f32[1,8,16,16,128]{4,0,3,2,1:T(1,128)}) fusion(bf16[1,8,16,16,128]{4,3,2,1,0:T(8,128)(2,1)S(1)} %copy-done.36, bf16[1,12,16,16,128]{4,0,3,2,1:T(2,128)(2,1)S(1)} %constant_dynamic-update-slice_fusion.3, bf16[3,3,3,128,128]{4,3,2,1,0:T(8,128)(2,1)S(1)} %copy-done), kind=kOutput, calls=%fused_computation.103 | convolution fusion | flops 1525153792 | bytes 4816896 | tf_op jit(solution)/shard_map/conv_general_dilated | solution.py:25
  121.2 6.0 %pad_slice_fusion.29 = (bf16[1,8,16,16,128]{4,0,3,2,1:T(2,128)(2,1)S(1)}, bf16[1,8,16,16,128]{4,0,3,2,1:T(2,128)(2,1)S(1)}, bf16[1,8,16,16,128]{4,0,3,2,1:T(2,12...) fusion(bf16[1,12,16,16,128]{4,0,3,2,1:T(2,128)(2,1)S(1)} %const, ...), kind=kLoop, calls=%fused_computation.322 | loop fusion | bytes 3932160 | tf_op jit(solution)/shard_map/slice | solution.py:51
  127.2 9.6 %pad_slice_fusion.38 = (bf16[1,8,16,16,128]{4,0,3,2,1:T(2,128)(2,1)S(1)}, bf16[1,8,16,16,128]{4,0,3,2,1:T(2,128)(2,1)S(1)}, bf16[1,8,16,16,128]{4,0,3,2,1:T(2,12...) fusion(bf16[1,12,16,16,128]{4,0,3,2,1:T(2,128)(2,1)S(1)} %const, ...), kind=kLoop, calls=%fused_computation.331 | loop fusion | bytes 5505024 | tf_op jit(solution)/shard_map/slice | solution.py:51
  136.8 9.7 %pad_slice_fusion.47 = (bf16[1,8,16,16,128]{4,0,3,2,1:T(2,128)(2,1)S(1)}, bf16[1,8,16,16,128]{4,0,3,2,1:T(2,128)(2,1)S(1)}, bf16[1,8,16,16,128]{4,0,3,2,1:T(2,12...) fusion(bf16[1,12,16,16,128]{4,0,3,2,1:T(2,128)(2,1)S(1)} %const, ...), kind=kLoop, calls=%fused_computation.340 | loop fusion | bytes 5505024 | tf_op jit(solution)/shard_map/slice | solution.py:51
  147.2 1.0 convolution_bitcast_fusion.13
  148.2 1.5 collective-permute-start.4
  149.7 1.5 collective-permute-start.5
  153.3 1.0 convolution_bitcast_fusion.16
  154.2 1.0 convolution_bitcast_fusion.15
  155.2 1.0 convolution_bitcast_fusion.14
  156.2 1.0 convolution_bitcast_fusion.11
  157.2 1.0 convolution_bitcast_fusion.10
  158.1 1.0 convolution_bitcast_fusion.9
  161.6 0.8 maximum_bitcast_fusion.21
  162.3 0.7 maximum_bitcast_fusion.23
  163.0 0.8 maximum_bitcast_fusion.15
  163.8 11.7 %fusion.9 = bf16[1,8,16,16,128]{4,0,3,2,1:T(2,128)(2,1)S(1)} fusion(bf16[3,3,3,128,128]{4,3,2,1,0:T(8,128)(2,1)S(1)} %copy-done, bf16[1,2,16,16,128]{4,0,3,2,1:T(2,128)(2,1)S(1)} %collective-permute-done.5, bf16[1,8,16,16,128]{4,0,3,2,1:T(2,128)(2,1)S(1)} %get-tuple-element.21, bf16[1,2,16,16,128]{4,0,3,2,1:T(2,128)(2,1)S(1)} %collective-permute-done.4), kind=kOutput, calls=%fused_computation.41 | convolution fusion | flops 1525153792 | bytes 2195456 | tf_op jit(solution)/shard_map/conv_general_dilated | solution.py:25
  175.6 11.5 %reduce.1 = bf16[2048,128]{1,0:T(8,128)(2,1)S(1)} reduce(bf16[2048,1,128]{2,1,0:T(2,128)(2,1)S(1)} %bitcast.647, bf16[]{:T(256)} %broadcast.79), dimensions={1}, to_apply=%bitcast.618.reduce_sub_computation | reduce | bytes 1048578
  187.1 0.9 reshape.488
  188.0 4.4 %all-to-all-start.2 = ((bf16[16,2,8192]{2,1,0:T(2,128)(2,1)}), bf16[16,2,8192]{2,1,0:T(2,128)(2,1)S(1)}, u32[]{:S(2)}, u32[]{:S(2)}) async-start(bf16[16,2,8192]{2,1,0:T(2,128)(2,1)} %reshape.488), calls=%async_computation.2 | async-start | bytes 1048576 | tf_op jit(solution)/shard_map/all_to_all | solution.py:81
  192.4 0.7 maximum_bitcast_fusion.20
  193.1 2.1 convolution_bitcast_fusion.12
  195.6 0.9 copy-done.8
  196.8 0.9 copy-done.7
  198.1 8.8 %all-to-all-done.2 = bf16[16,2,8192]{2,1,0:T(2,128)(2,1)S(1)} async-done(((bf16[16,2,8192]{2,1,0:T(2,128)(2,1)}), bf16[16,2,8192]{2,1,0:T(2,128)(2,1)S(1)}, u32[]{:S(2)}, u32[]{:S(2)}) %all-to-all-start.2) | async-done | bytes 524320 | tf_op jit(solution)/shard_map/all_to_all | solution.py:81
  207.5 0.6 gather_fusion.1
  208.1 1.1 add_convert_fusion
  209.3 4.1 %all-to-all-start.3 = ((bf16[16,128,128]{2,1,0:T(8,128)(2,1)}), bf16[16,128,128]{2,1,0:T(8,128)(2,1)S(1)}, u32[]{:S(2)}, u32[]{:S(2)}) async-start(bf16[16,128,128]{2,1,0:T(8,128)(2,1)} %add_convert_fusion), calls=%async_computation.3 | async-start | bytes 1048576 | tf_op jit(solution)/shard_map/all_to_all | solution.py:85
  213.7 1.7 convolution_bitcast_fusion.17
  215.6 0.8 copy-done.17
  216.6 1.4 pad_maximum_fusion.1
  218.0 9.8 %all-to-all-done.3 = bf16[16,128,128]{2,1,0:T(8,128)(2,1)S(1)} async-done(((bf16[16,128,128]{2,1,0:T(8,128)(2,1)}), bf16[16,128,128]{2,1,0:T(8,128)(2,1)S(1)}, u32[]{:S(2)}, u32[]{:S(2)}) %all-to-all-start.3) | async-done | bytes 524320 | tf_op jit(solution)/shard_map/all_to_all | solution.py:85
  228.3 0.7 copy-done.12
  237.6 0.7 copy-done.10
  239.3 0.7 copy-done.28
  240.4 1.4 pad_maximum_fusion
  241.8 1.2 copy-done.4
  243.3 1.1 multiply_convert_fusion.1
  244.4 0.9 copy.182
  245.3 136.7 %all-reduce.5.cloned.1.call-done = (f32[3,3,3,128,128]{4,3,2,1,0:T(8,128)}, f32[3,3,3,128,128]{4,3,2,1,0:T(8,128)}) async-done(((f32[3,3,3,128,128]{4,3,2,1,0:T(8,128)}, f32[3,3,3,128,128]{4,3,2,1,0:T(8,128)}), (f32[3,3,3,128,128]{4,3,2,1,0:T(8,128)}, f32[3,3,3,128,128]{4,3,2,1,0:T(8,128)})) %all-reduce.5.cloned.1.call-update) | async-done | bytes 3538960 | tf_op jit(solution)/shard_map/psum | solution.py:123
  382.0 3.0 copy.435
  385.0 1.2 copy.436
  (163 shorter events, 23.3 us)
Async XLA Ops:
  7.2 97.2 %copy-start = (bf16[3,3,3,128,128]{4,3,2,1,0:T(8,128)(2,1)S(1)}, bf16[3,3,3,128,128]{4,3,2,1,0:T(8,128)(2,1)}, u32[]{:S(2)}) copy-start(bf16[3,3,3,128,128]{4,3,2,1,0:T(8,128)(2,1)} %param.10) | copy-start | bytes 2654212
  8.1 6.8 %collective-permute-start = (bf16[1,1,16,16,128]{4,3,2,1,0:T(8,128)(2,1)S(1)}, bf16[1,1,16,16,128]{4,3,2,1,0:T(8,128)(2,1)S(1)}, u32[]{:S(2)}, u32[]{:S(2)}) collective-permute-start(bf16[1,1,16,16,128]{4,3,2,1,0:T(8,128)(2,1)S(1)} %get-tuple-element.54), channel_id=1, source_target_pairs={{0,1},{2,3},{4,5},{6,7},{8,9},{10,11},{12,13},{14,15},{16,17},{18,... | collective-permute-start | bytes 196616 | tf_op jit(solution)/shard_map/ppermute | solution.py:15
  13.0 6.2 %collective-permute-start.1 = (bf16[1,1,16,16,128]{4,3,2,1,0:T(8,128)(2,1)S(1)}, bf16[1,1,16,16,128]{4,3,2,1,0:T(8,128)(2,1)S(1)}, u32[]{:S(2)}, u32[]{:S(2)}) collective-permute-start(bf16[1,1,16,16,128]{4,3,2,1,0:T(8,128)(2,1)S(1)} %get-tuple-element.53), channel_id=1, source_target_pairs={{1,0},{3,2},{5,4},{7,6},{9,8},{11,10},{13,12},{15,14},{17,16},{19,... | collective-permute-start | bytes 196616 | tf_op jit(solution)/shard_map/ppermute | solution.py:17
  14.9 0.6 copy-start.27
  19.2 0.6 copy-start.29
  19.8 0.9 copy-start.11
  21.0 1.2 copy-start.35
  21.0 1.2 copy-start.38
  38.6 18.3 %copy-start.37 = (s32[16]{0:T(128)S(1)}, s32[16]{0:T(128)}, u32[]{:S(2)}) copy-start(s32[16]{0:T(128)} %param.11) | copy-start | bytes 196
  38.6 18.4 %copy-start.34 = (f32[16]{0:T(128)S(1)}, f32[16]{0:T(128)}, u32[]{:S(2)}) copy-start(f32[16]{0:T(128)} %param.12) | copy-start | bytes 196
  51.0 20.4 %all-to-all-start = ((bf16[16,2,8192]{2,1,0:T(2,128)(2,1)}), bf16[16,2,8192]{2,1,0:T(2,128)(2,1)S(1)}, u32[]{:S(2)}, u32[]{:S(2)}) async-start(bf16[16,2,8192]{2,1,0:T(2,128)(2,1)} %reshape.486), calls=%async_computation | async-start | bytes 1048576 | tf_op jit(solution)/shard_map/all_to_all | solution.py:81
  72.6 21.0 %copy-start.3 = (f32[8,16,8,3,128]{4,2,3,1,0:T(8,128)S(1)}, f32[8,16,8,3,128]{4,2,3,1,0:T(8,128)}, u32[]{:S(2)}) copy-start(f32[8,16,8,3,128]{4,2,3,1,0:T(8,128)} %get-tuple-element.23) | copy-start | bytes 4718596
  91.7 7.5 %collective-permute-start.2 = (bf16[1,2,16,16,128]{4,0,3,2,1:T(2,128)(2,1)S(1)}, bf16[1,2,16,16,128]{4,0,3,2,1:T(2,128)(2,1)S(1)}, u32[]{:S(2)}, u32[]{:S(2)}) collective-permute-start(bf16[1,2,16,16,128]{4,0,3,2,1:T(2,128)(2,1)S(1)} %copy.425), channel_id=1, source_target_pairs={{0,1},{2,3},{4,5},{6,7},{8,9},{10,11},{12,13},{14,15},{16,17},{18,... | collective-permute-start | bytes 393224 | tf_op jit(solution)/shard_map/ppermute | solution.py:15
  94.0 10.4 %copy-start.36 = (bf16[1,8,16,16,128]{4,3,2,1,0:T(8,128)(2,1)S(1)}, bf16[1,8,16,16,128]{4,3,2,1,0:T(8,128)(2,1)}, u32[]{:S(2)}) copy-start(bf16[1,8,16,16,128]{4,3,2,1,0:T(8,128)(2,1)} %param.13) | copy-start | bytes 1572868
  94.2 9.8 %collective-permute-start.3 = (bf16[1,2,16,16,128]{4,0,3,2,1:T(2,128)(2,1)S(1)}, bf16[1,2,16,16,128]{4,0,3,2,1:T(2,128)(2,1)S(1)}, u32[]{:S(2)}, u32[]{:S(2)}) collective-permute-start(bf16[1,2,16,16,128]{4,0,3,2,1:T(2,128)(2,1)S(1)} %copy.426), channel_id=1, source_target_pairs={{1,0},{3,2},{5,4},{7,6},{9,8},{11,10},{13,12},{15,14},{17,16},{19,... | collective-permute-start | bytes 393224 | tf_op jit(solution)/shard_map/ppermute | solution.py:17
  120.6 40.6 %copy-start.19 = (bf16[1,8,16,16,128]{4,3,0,2,1:T(8,128)(2,1)}, bf16[1,8,16,16,128]{4,3,0,2,1:T(8,128)(2,1)S(1)}, u32[]{:S(2)}) copy-start(bf16[1,8,16,16,128]{4,3,0,2,1:T(8,128)(2,1)S(1)} %copy.241) | copy-start | bytes 1572868
  148.2 15.6 %collective-permute-start.4 = (bf16[1,2,16,16,128]{4,0,3,2,1:T(2,128)(2,1)S(1)}, bf16[1,2,16,16,128]{4,0,3,2,1:T(2,128)(2,1)S(1)}, u32[]{:S(2)}, u32[]{:S(2)}) collective-permute-start(bf16[1,2,16,16,128]{4,0,3,2,1:T(2,128)(2,1)S(1)} %get-tuple-element.49), channel_id=1, source_target_pairs={{0,1},{2,3},{4,5},{6,7},{8,9},{10,11},{12,13},{14,15},{16,17},{18,... | collective-permute-start | bytes 393224 | tf_op jit(solution)/shard_map/ppermute | solution.py:15
  149.7 14.2 %collective-permute-start.5 = (bf16[1,2,16,16,128]{4,0,3,2,1:T(2,128)(2,1)S(1)}, bf16[1,2,16,16,128]{4,0,3,2,1:T(2,128)(2,1)S(1)}, u32[]{:S(2)}, u32[]{:S(2)}) collective-permute-start(bf16[1,2,16,16,128]{4,0,3,2,1:T(2,128)(2,1)S(1)} %get-tuple-element.50), channel_id=1, source_target_pairs={{1,0},{3,2},{5,4},{7,6},{9,8},{11,10},{13,12},{15,14},{17,16},{19,... | collective-permute-start | bytes 393224 | tf_op jit(solution)/shard_map/ppermute | solution.py:17
  175.6 16.8 %copy-start.31 = (f32[1,128,128]{2,1,0:T(8,128)S(1)}, f32[1,128,128]{2,1,0:T(8,128)}, u32[]{:S(2)}) copy-start(f32[1,128,128]{2,1,0:T(8,128)} %convolution_bitcast_fusion.11) | copy-start | bytes 196612
  175.6 16.8 %copy-start.32 = (f32[1,128,128]{2,1,0:T(8,128)S(1)}, f32[1,128,128]{2,1,0:T(8,128)}, u32[]{:S(2)}) copy-start(f32[1,128,128]{2,1,0:T(8,128)} %convolution_bitcast_fusion.10) | copy-start | bytes 196612
  175.6 16.8 %copy-start.33 = (f32[1,128,128]{2,1,0:T(8,128)S(1)}, f32[1,128,128]{2,1,0:T(8,128)}, u32[]{:S(2)}) copy-start(f32[1,128,128]{2,1,0:T(8,128)} %convolution_bitcast_fusion.9) | copy-start | bytes 196612
  187.1 6.0 %copy-start.6 = (bf16[1,8,16,16,128]{4,0,3,2,1:T(2,128)(2,1)S(1)}, bf16[1,8,16,16,128]{4,0,3,2,1:T(2,128)(2,1)}, u32[]{:S(2)}) copy-start(bf16[1,8,16,16,128]{4,0,3,2,1:T(2,128)(2,1)} %get-tuple-element.37) | copy-start | bytes 1572868
  188.0 18.9 %all-to-all-start.2 = ((bf16[16,2,8192]{2,1,0:T(2,128)(2,1)}), bf16[16,2,8192]{2,1,0:T(2,128)(2,1)S(1)}, u32[]{:S(2)}, u32[]{:S(2)}) async-start(bf16[16,2,8192]{2,1,0:T(2,128)(2,1)} %reshape.488), calls=%async_computation.2 | async-start | bytes 1048576 | tf_op jit(solution)/shard_map/all_to_all | solution.py:81
  193.1 2.1 copy-start.9
  193.1 2.1 copy-start.20
  195.3 1.2 copy-start.8
  196.5 1.2 copy-start.7
  208.1 5.5 %copy-start.21 = (bf16[1,8,16,16,128]{4,3,0,2,1:T(8,128)(2,1)S(1)}, bf16[1,8,16,16,128]{4,3,0,2,1:T(8,128)(2,1)}, u32[]{:S(2)}) copy-start(bf16[1,8,16,16,128]{4,3,0,2,1:T(8,128)(2,1)} %copy-done.19) | copy-start | bytes 1572868
  209.3 18.6 %all-to-all-start.3 = ((bf16[16,128,128]{2,1,0:T(8,128)(2,1)}), bf16[16,128,128]{2,1,0:T(8,128)(2,1)S(1)}, u32[]{:S(2)}, u32[]{:S(2)}) async-start(bf16[16,128,128]{2,1,0:T(8,128)(2,1)} %add_convert_fusion), calls=%async_computation.3 | async-start | bytes 1048576 | tf_op jit(solution)/shard_map/all_to_all | solution.py:85
  213.4 168.7 %all-reduce.5.cloned.1.call-start = ((), (), s32[]{:S(2)}) async-start(), calls=%async_computation.4 | async-start | bytes 7077888 | tf_op jit(solution)/shard_map/psum | solution.py:123
  213.6 1.8 copy-start.22
  213.6 1.8 copy-start.23
  213.6 1.8 copy-start.24
  213.6 1.8 copy-start.25
  213.7 1.8 copy-start.26
  213.7 1.8 copy-start.13
  213.7 1.8 copy-start.15
  213.7 1.8 copy-start.16
  215.4 0.9 copy-start.17
  215.4 1.0 copy-start.18
  215.4 1.1 copy-start.14
  227.9 1.1 copy-start.12
  237.3 1.0 copy-start.10
  237.6 1.1 copy-start.30
  239.1 0.8 copy-start.28
  241.8 1.2 copy-start.4
  241.8 1.5 copy-start.5
  382.0 3.0 copy-start.2
  382.0 4.2 %copy-start.1 = (bf16[3,3,3,128,128]{4,3,2,1,0:T(8,128)(2,1)S(1)}, bf16[3,3,3,128,128]{4,3,2,1,0:T(8,128)(2,1)}, u32[]{:S(2)}) copy-start(bf16[3,3,3,128,128]{4,3,2,1,0:T(8,128)(2,1)} %param.10) | copy-start | bytes 2654212
Sparse Core Ops, SparseCore 0:
  241.9 140.0 all-reduce.4
where the time goes:
time: 400 us; the launch traced here: 393 us
  waiting for transfers between devices  180 us (45%)
  matrix products  61.7 us (15%)
  local copies, waits for them, and re-layouts  58.8 us (15%)
  other arithmetic  32.1 us (8%)
  starting transfers between devices  26.7 us (7%)
  blocking collectives  18.5 us (5%)
  between operations  15.3 us (4%)
    psum x1, waiting for transfers between devices, shards(): lax.psum((first_local, second_local), ('sample', 'space'))  137 us
    conv_general_dilated x3, matrix products, convolve(): lax.conv_general_dilated(volume_in, kernel, (1, 1, 1), ((0, 0), (spread,...  35.2 us
    dot_general x54, matrix products, kernel_grad(): lax.dot_general(window.reshape(-1, framed.shape[4]), flat_cotangent, (((0...  26.3 us
    slice x3, local copies, waits for them, and re-layouts, kernel_grad(): lax.slice(framed, (0, depth_tap * spread, row_tap * spread, col_tap * spr...  25.3 us
    all_to_all x2, waiting for transfers between devices, to_pieces(): lax.all_to_all(flat, 'sample', split_axis=1, concat_axis=0, tiled=True)  23.2 us
    unnamed x2, other arithmetic  23 us
    unnamed x96, local copies, waits for them, and re-layouts  20.9 us
    all_to_all x1, blocking collectives, to_slabs(): lax.all_to_all(pieces, 'sample', split_axis=0, concat_axis=1, tiled=True)  18.5 us
  transfers between devices with their start and end apart: 10, of which 8 were waited for; matrix products, arithmetic and copies ran while one was open for 6% of the time, Pallas kernels for 0%

commit v1 on v0

v1 whole, which is shorter than its diff:
```python
import functools

import jax
import jax.numpy as jnp
from jax import lax
from jax.experimental import pallas as pl
from jax.experimental.pallas import tpu as pltpu
from jax.sharding import PartitionSpec as P

F32 = jnp.float32
BF16 = jnp.bfloat16
VMEM_LIMIT = 56 * 1024 * 1024


def slope(value):
    squash = jax.nn.sigmoid(value)
    return squash * (1.0 + value * (1.0 - squash))


def groups(depth, spread):
    first = [p for p in range(depth) if (p // spread) % 2 == 0]
    return first, [p + spread for p in first]


def frame(store, layer, plane, spread, width):
    cells, chans = plane.shape
    edge = spread * width
    wide = plane.astype(F32)
    column = lax.broadcasted_iota(jnp.int32, plane.shape, 0) % width
    left = jnp.where(column >= spread, pltpu.roll(wide, spread, 0), 0.0).astype(BF16)
    right = jnp.where(column < width - spread, pltpu.roll(wide, cells - spread, 0), 0.0).astype(BF16)
    store[layer, pl.ds(0, edge), :] = jnp.zeros((edge, 3 * chans), BF16)
    store[layer, pl.ds(edge + cells, edge), :] = jnp.zeros((edge, 3 * chans), BF16)
    for place, value in enumerate((left, plane, right)):
        store[layer, pl.ds(edge, cells), pl.ds(place * chans, chans)] = value


def taps(store, layer, spread, width, cells):
    return jnp.concatenate(
        [store[layer, pl.ds(row * spread * width, cells), :] for row in range(3)], axis=1
    )


def fill_pairs(kernel_ref, wide_ref):
    chans = kernel_ref.shape[2]
    for step in range(4):
        for out in range(2):
            depth_tap = step - out
            block = (
                kernel_ref[depth_tap]
                if 0 <= depth_tap < 3
                else jnp.zeros(kernel_ref.shape[1:], BF16)
            )
            wide_ref[step, :, pl.ds(out * chans, chans)] = block


def conv_pairs(store, wide_ref, depth, spread, width, cells):
    chans = wide_ref.shape[2] // 2
    first, _ = groups(depth, spread)
    total = None
    for half in range(2):
        rows = []
        for p in first:
            rows.append(
                jnp.concatenate(
                    [
                        taps(store, p + spread * (2 * half + k), spread, width, cells)
                        for k in range(2)
                    ],
                    axis=1,
                )
            )
        lhs = jnp.concatenate(rows, axis=0)
        rhs = jnp.concatenate([wide_ref[2 * half], wide_ref[2 * half + 1]], axis=0)
        part = jnp.dot(lhs, rhs, preferred_element_type=F32)
        total = part if total is None else total + part
    for place, p in enumerate(first):
        for out in range(2):
            yield p + out * spread, total[
                place * cells : (place + 1) * cells, out * chans : (out + 1) * chans
            ]


def grad_blocks(store, grad_at, depth, spread, width, cells):
    ranges = ((0, 2 * spread, (0, 1)), (2 * spread, depth, (0, 1, 2)), (depth, depth + 2 * spread, (1, 2)))
    for low, high, depth_taps in ranges:
        lhs = jnp.concatenate(
            [taps(store, e, spread, width, cells) for e in range(low, high)], axis=0
        )
        columns = []
        for tap in depth_taps:
            layers = []
            for e in range(low, high):
                p = e - spread * tap
                layers.append(grad_at(p if 0 <= p < depth else None))
            columns.append(jnp.concatenate(layers, axis=0))
        rhs = jnp.concatenate(columns, axis=1)
        part = lax.dot_general(lhs, rhs, (((0,), (0,)), ((), ())), preferred_element_type=F32)
        chans = columns[0].shape[1]
        for place, tap in enumerate(depth_taps):
            yield tap, part[:, place * chans : (place + 1) * chans]


def first_kernel_body(width, share_ref, x_ref, kernel_ref, hidden_ref, slope_ref, store, wide_ref):
    depth, cells, _ = hidden_ref.shape
    for layer in range(depth + 2):
        frame(store, layer, x_ref[layer], 1, width)
    fill_pairs(kernel_ref, wide_ref)
    for p, value in conv_pairs(store, wide_ref, depth, 1, width, cells):
        squash = jax.nn.sigmoid(value)
        hidden_ref[p] = (value * squash).astype(BF16)
        slope_ref[p] = share_ref[0] * (squash * (1.0 + value * (1.0 - squash)))


def mix_body(width, share_ref, x_ref, kernel_ref, own_ref, mixed_ref, slope_ref, store, wide_ref):
    depth, cells, _ = mixed_ref.shape
    for layer in range(depth + 2):
        frame(store, layer, x_ref[layer], 1, width)
    fill_pairs(kernel_ref, wide_ref)
    for p, value in conv_pairs(store, wide_ref, depth, 1, width, cells):
        squash = jax.nn.sigmoid(value)
        hidden = (value * squash).astype(BF16).astype(F32)
        mixed_ref[p] = (share_ref[0] * own_ref[p].astype(F32) + share_ref[1] * hidden).astype(BF16)
        slope_ref[p] = share_ref[1] * (squash * (1.0 + value * (1.0 - squash)))


def second_body(width, low_ref, mixed_ref, high_ref, kernel_ref, cot_ref, result_ref, grad_ref, store, wide_ref):
    depth, cells, _ = result_ref.shape
    for layer in range(depth + 4):
        plane = (
            low_ref[layer]
            if layer < 2
            else (mixed_ref[layer - 2] if layer < depth + 2 else high_ref[layer - depth - 2])
        )
        frame(store, layer, plane, 2, width)
    fill_pairs(kernel_ref, wide_ref)
    for p, value in conv_pairs(store, wide_ref, depth, 2, width, cells):
        squash = jax.nn.sigmoid(value)
        result_ref[p] = (value * squash).astype(BF16)
        grad_ref[p] = (
            cot_ref[p].astype(F32) * (squash * (1.0 + value * (1.0 - squash)))
        ).astype(BF16)


def second_grad_body(width, low_ref, mixed_ref, high_ref, grad_ref, out_ref, store, total):
    depth, cells, chans = grad_ref.shape
    for layer in range(depth + 4):
        plane = (
            low_ref[layer]
            if layer < 2
            else (mixed_ref[layer - 2] if layer < depth + 2 else high_ref[layer - depth - 2])
        )
        frame(store, layer, plane, 2, width)

    def grad_at(p):
        return jnp.zeros((cells, chans), BF16) if p is None else grad_ref[p]

    total[...] = jnp.zeros_like(total)
    for tap, part in grad_blocks(store, grad_at, depth, 2, width, cells):
        total[tap] += part
    out_ref[...] = total[...].astype(BF16)


def back_body(
    width, low_ref, grad_ref, high_ref, kernel_ref, slope_own_ref, slope_mate_ref, own_ref, mate_ref,
    out_ref, store, wide_ref, term_own, term_mate, store_one, total,
):
    depth, cells, chans = grad_ref.shape
    for layer in range(depth + 4):
        plane = (
            low_ref[layer]
            if layer < 2
            else (grad_ref[layer - 2] if layer < depth + 2 else high_ref[layer - depth - 2])
        )
        frame(store, layer, plane, 2, width)
    fill_pairs(kernel_ref, wide_ref)
    for p, value in conv_pairs(store, wide_ref, depth, 2, width, cells):
        value = value.astype(BF16).astype(F32)
        term_own[p] = (value * slope_own_ref[p]).astype(BF16)
        term_mate[p] = (value * slope_mate_ref[p]).astype(BF16)
    total[...] = jnp.zeros_like(total)
    for x_ref, term in ((own_ref, term_own), (mate_ref, term_mate)):
        for layer in range(depth + 2):
            frame(store_one, layer, x_ref[layer], 1, width)

        def grad_at(p, term=term):
            return jnp.zeros((cells, chans), BF16) if p is None else term[p]

        for tap, part in grad_blocks(store_one, grad_at, depth, 1, width, cells):
            total[tap] += part
    out_ref[...] = total[...].astype(BF16)


def call(body, width, args, outs, scratch, flops, smem=0):
    vmem = pl.BlockSpec(memory_space=pltpu.VMEM)
    scalar = pl.BlockSpec(memory_space=pltpu.SMEM)
    size = sum(a.size * a.dtype.itemsize for a in args)
    return pl.pallas_call(
        functools.partial(body, width),
        out_shape=outs,
        in_specs=[scalar] * smem + [vmem] * (len(args) - smem),
        out_specs=jax.tree.map(lambda _: vmem, outs),
        scratch_shapes=scratch,
        compiler_params=pltpu.CompilerParams(vmem_limit_bytes=VMEM_LIMIT),
        cost_estimate=pl.CostEstimate(flops=flops, bytes_accessed=size, transcendentals=0),
    )(*args)


def edges(block, width):
    count = lax.axis_size("space")
    low = lax.ppermute(block[-width:], "space", [(i, i + 1) for i in range(count - 1)])
    high = lax.ppermute(block[:width], "space", [(i + 1, i) for i in range(count - 1)])
    return low, high


def shards(volume, first_kernel, second_kernel, partner, coefficient, out_grad):
    _, depth, height, width, chans = volume.shape
    cells = height * width
    me = lax.axis_index("sample")
    own_share = coefficient[me]
    shares = jnp.stack([own_share, 1.0 - own_share])
    x = volume.reshape(depth, cells, chans)
    cot = out_grad.reshape(depth, cells, chans)
    flat_one = first_kernel.reshape(3, 9 * chans, chans)
    flat_two = second_kernel.reshape(3, 9 * chans, chans)
    flipped = jnp.transpose(jnp.flip(second_kernel, (0, 1, 2)), (0, 1, 2, 4, 3)).reshape(
        3, 9 * chans, chans
    )
    count = lax.axis_size("sample")
    pieces = lax.all_to_all(
        x.reshape(count, depth * cells // count, chans), "sample", split_axis=0, concat_axis=0, tiled=True
    )
    mate = lax.all_to_all(
        jnp.take(pieces, partner, axis=0), "sample", split_axis=0, concat_axis=0, tiled=True
    ).reshape(depth, cells, chans)
    low, high = edges(x, 1)
    own_pad = jnp.concatenate([low, x, high], axis=0)
    low, high = edges(mate, 1)
    mate_pad = jnp.concatenate([low, mate, high], axis=0)
    layer = (depth, cells, chans)
    half = jax.ShapeDtypeStruct(layer, BF16)
    full = jax.ShapeDtypeStruct(layer, F32)
    unit = 2 * depth * cells * 27 * chans * chans
    store_one = pltpu.VMEM((depth + 2, cells + 2 * width, 3 * chans), BF16)
    store_two = pltpu.VMEM((depth + 4, cells + 4 * width, 3 * chans), BF16)
    wide = pltpu.VMEM((4, 9 * chans, 2 * chans), BF16)
    total = pltpu.VMEM((3, 9 * chans, chans), F32)
    hidden, slope_own = call(
        first_kernel_body, width, (shares, own_pad, flat_one), (half, full), [store_one, wide], unit, 1
    )
    mixed, slope_mate = call(
        mix_body, width, (shares, mate_pad, flat_one, hidden), (half, full), [store_one, wide], unit, 1
    )
    low, high = edges(mixed, 2)
    result, grad_two = call(
        second_body, width, (low, mixed, high, flat_two, cot), (half, half), [store_two, wide], unit
    )
    terms = jax.ShapeDtypeStruct((3, 9 * chans, chans), BF16)
    second_local = call(
        second_grad_body, width, (low, mixed, high, grad_two), terms, [store_two, total], unit
    )
    low, high = edges(grad_two, 2)
    first_local = call(
        back_body,
        width,
        (low, grad_two, high, flipped, slope_own, slope_mate, own_pad, mate_pad),
        terms,
        [store_two, wide, pltpu.VMEM(layer, BF16), pltpu.VMEM(layer, BF16), store_one, total],
        3 * unit,
    )
    shape = first_kernel.shape
    second_sum = lax.psum(second_local, ("sample", "space")).astype(F32).reshape(shape)
    first_sum = lax.psum(first_local, ("sample", "space")).astype(F32).reshape(shape)
    return result.reshape(volume.shape), first_sum, second_sum


def solution(mesh):
    in_specs = (
        P("sample", "space", None, None, None),
        P(),
        P(),
        P(),
        P(),
        P("sample", "space", None, None, None),
    )
    out_specs = (P("sample", "space", None, None, None), P(), P())
    return jax.shard_map(shards, mesh=mesh, in_specs=in_specs, out_specs=out_specs, check_vma=False)
```

time: 400 us -> 254 us (0.64); the launches traced: 393 us -> 253 us
  matrix products: 61.7 us -> 0 us
  local copies, waits for them, and re-layouts: 58.8 us -> 6.3 us
  Pallas kernels: 0 us -> 38.5 us
  waiting for transfers between devices: 180 us -> 155 us
  other arithmetic: 32.1 us -> 9.5 us
  blocking collectives: 18.5 us -> 0 us
    pallas_call x0 -> x5, Pallas kernels: none -> 38.5 us  [call(): pl.pallas_call(functools.partial(body, width), out_shape=outs, in_specs=[...]
    conv_general_dilated x3 -> x0, matrix products: 35.2 us -> none  [convolve(): lax.conv_general_dilated(volume_in, kernel, (1, 1, 1), ((0, 0), (spread,...]
    dot_general x55 -> x0, matrix products: 26.5 us -> none  [the longest x54 26.3 us: kernel_grad(): lax.dot_general(window.reshape(-1, framed.shape[4]), flat_cotangent, (((0...]
    slice x6 -> x4, local copies, waits for them, and re-layouts: 26.8 us -> 1.99 us  [the longest x2 1.97 us: edges(): block[:width]]
    unnamed x2 -> x0, other arithmetic: 23 us -> none
    unnamed x96 -> x16, local copies, waits for them, and re-layouts: 20.9 us -> 1.33 us
    all_to_all x1 -> x0, blocking collectives: 18.5 us -> none  [to_slabs(): lax.all_to_all(pieces, 'sample', split_axis=0, concat_axis=1, tiled=True)]
    all_to_all x3 -> x2, waiting for transfers between devices: 33 us -> 18.1 us  [the longest x1 13.1 us: shards(): lax.all_to_all(x.reshape(count, depth * cells // count, chans), 'sample',...]
  transfers between devices with their start and end apart: 10 -> 11, of which waited for: 8 -> 5; matrix products, arithmetic and copies ran while one was open for 6% -> 2% of each run, Pallas kernels for 0% -> 4%
where the time goes in v1:
time: 254 us; the launch traced here: 253 us
  waiting for transfers between devices  155 us (61%)
  Pallas kernels  38.5 us (15%)
  starting transfers between devices  28.7 us (11%)
  between operations  14.9 us (6%)
  other arithmetic  9.5 us (4%)
  local copies, waits for them, and re-layouts  6.3 us (2%)
    psum x1, waiting for transfers between devices, shards(): lax.psum(first_local, ('sample', 'space')).astype(F32).reshape(shape)  133 us
    pallas_call x5, Pallas kernels, call(): pl.pallas_call(functools.partial(body, width), out_shape=outs, in_specs=[...  38.5 us
    all_to_all x1, waiting for transfers between devices, shards(): lax.all_to_all(x.reshape(count, depth * cells // count, chans), 'sample',...  13.1 us
    ppermute x4, starting transfers between devices, edges(): lax.ppermute(block[-width:], 'space', [(i, i + 1) for i in range(count -...  11.9 us
    all_to_all x1, starting transfers between devices, shards(): lax.all_to_all(x.reshape(count, depth * cells // count, chans), 'sample',...  7.37 us
    ppermute x4, starting transfers between devices, edges(): lax.ppermute(block[:width], 'space', [(i + 1, i) for i in range(count - 1)])  5.35 us
  transfers between devices with their start and end apart: 11, of which 5 were waited for; matrix products, arithmetic and copies ran while one was open for 2% of the time, Pallas kernels for 4%

profile of v1, /device:TPU:0, one launch (start us, length us, event | category | flops | bytes accessed | tf_op | source)
XLA Modules:
  0.0 253.1 jit_solution(15362062693195062671)
XLA Ops:
  7.2 7.4 %all-to-all-start = ((bf16[16,128,128]{2,1,0:T(8,128)(2,1)}), bf16[16,128,128]{2,1,0:T(8,128)(2,1)S(1)}, u32[]{:S(2)}, u32[]{:S(2)}) async-start(bf16[16,128,128]{2,1,0:T(8,128)(2,1)} %bitcast.16), calls=%async_computation | async-start | bytes 1048576 | tf_op jit(solution)/shard_map/all_to_all | solution.py:230
  14.5 0.0 copy-start
  14.6 0.0 copy-start.7
  14.6 0.7 compare_select_fusion
  15.3 0.7 compare_and_fusion
  15.9 13.1 %all-to-all-done = bf16[16,128,128]{2,1,0:T(8,128)(2,1)S(1)} async-done(((bf16[16,128,128]{2,1,0:T(8,128)(2,1)}), bf16[16,128,128]{2,1,0:T(8,128)(2,1)S(1)}, u32[]{:S(2)}, u32[]{:S(2)}) %all-to-all-start) | async-done | bytes 524320 | tf_op jit(solution)/shard_map/all_to_all | solution.py:230
  29.0 0.6 gather_fusion
  29.7 0.9 broadcast_select_fusion
  30.6 4.1 %all-to-all-start.1 = ((bf16[16,128,128]{2,1,0:T(8,128)(2,1)}), bf16[16,128,128]{2,1,0:T(8,128)(2,1)S(1)}, u32[]{:S(2)}, u32[]{:S(2)}) async-start(bf16[16,128,128]{2,1,0:T(8,128)(2,1)} %broadcast_select_fusion), calls=%async_computation.1 | async-start | bytes 1048576 | tf_op jit(solution)/shard_map/all_to_all | solution.py:233
  34.7 0.0 all-reduce.3.cloned.1.call-start
  34.7 0.0 copy-done
  34.8 1.3 collective-permute-start.3
  36.1 4.5 %collective-permute-start.2 = (bf16[1,256,128]{2,1,0:T(8,128)(2,1)S(1)}, bf16[1,256,128]{2,1,0:T(8,128)(2,1)S(1)}, u32[]{:S(2)}, u32[]{:S(2)}) collective-permute-start(bf16[1,256,128]{2,1,0:T(8,128)(2,1)S(1)} %bitcast.23), channel_id=1, source_target_pairs={{0,1},{2,3},{4,5},{6,7},{8,9},{10,11},{12,13},{14,15},{16,17},{18,... | collective-permute-start | bytes 196616 | tf_op jit(solution)/shard_map/ppermute | solution.py:211
  40.6 0.0 copy-done.7
  40.6 0.6 dynamic_slice.3
  41.9 1.3 pad_maximum_fusion.2.share_ref
  43.2 0.0 collective-permute-done.3
  43.2 0.0 collective-permute-done.2
  43.2 0.9 pad_maximum_fusion.1.x_ref.own_ref
  44.1 5.0 %all-to-all-done.1 = bf16[16,128,128]{2,1,0:T(8,128)(2,1)S(1)} async-done(((bf16[16,128,128]{2,1,0:T(8,128)(2,1)}), bf16[16,128,128]{2,1,0:T(8,128)(2,1)S(1)}, u32[]{:S(2)}, u32[]{:S(2)}) %all-to-all-start.1) | async-done | bytes 524320 | tf_op jit(solution)/shard_map/all_to_all | solution.py:233
  49.2 1.3 collective-permute-start.1
  50.5 4.5 %collective-permute-start = (bf16[1,256,128]{2,1,0:T(8,128)(2,1)S(1)}, bf16[1,256,128]{2,1,0:T(8,128)(2,1)S(1)}, u32[]{:S(2)}, u32[]{:S(2)}) collective-permute-start(bf16[1,256,128]{2,1,0:T(8,128)(2,1)S(1)} %bitcast.25), channel_id=1, source_target_pairs={{0,1},{2,3},{4,5},{6,7},{8,9},{10,11},{12,13},{14,15},{16,17},{18,... | collective-permute-start | bytes 196616 | tf_op jit(solution)/shard_map/ppermute | solution.py:211
  55.0 5.5 %shard_map.85 = (bf16[8,256,128]{2,1,0:T(8,128)(2,1)}, f32[8,256,128]{2,1,0:T(8,128)}) custom-call(f32[2]{0:T(128)} %pad_maximum_fusion.2.share_ref, bf16[10,256,128]{2,1,0:T(8,128)(2,1)} %pad_maximum_fusion.1.x_ref.own_ref, bf16[3,1152,128]{2,1,0:T(8,128)(2,1)} %bitcast.27), custom_call_target="tpu_custom_call" | custom-call | flops 1811939328 | bytes 1540104 | tf_op jit(solution)/shard_map/pallas_call | solution.py:198
  60.5 0.0 collective-permute-done.1
  60.5 0.0 collective-permute-done
  60.5 0.9 pad_maximum_fusion.x_ref.mate_ref
  61.4 0.0 copy-start.1
  61.4 5.9 %shard_map.86 = (bf16[8,256,128]{2,1,0:T(8,128)(2,1)}, f32[8,256,128]{2,1,0:T(8,128)}) custom-call(f32[2]{0:T(128)} %pad_maximum_fusion.2.share_ref, bf16[10,256,128]{2,1,0:T(8,128)(2,1)} %pad_maximum_fusion.x_ref.mate_ref, bf16[3,1152,128]{2,1,0:T(8,128)(2,1)} %bitcast.28, bf16[8,256,128]{2,1,0:T(8,128)(2,1)} %get-tuple-element.9.own_ref), custom_call_target="tpu_custom_call" | custom-call | flops 1811939328 | bytes 2064392 | tf_op jit(solution)/shard_map/pallas_call | solution.py:198
  67.3 1.0 fusion.1
  68.3 1.3 collective-permute-start.4
  69.6 1.3 collective-permute-start.5
  70.9 0.0 copy-done.1
  70.9 0.1 reverse_bitcast_fusion
  71.0 1.7 copy.9
  72.7 0.0 collective-permute-done.4.low_ref
  72.7 0.0 copy-start.3
  72.7 3.8 %collective-permute-done.5.high_ref = bf16[2,256,128]{2,1,0:T(8,128)(2,1)S(1)} collective-permute-done((bf16[2,256,128]{2,1,0:T(8,128)(2,1)S(1)}, bf16[2,256,128]{2,1,0:T(8,128)(2,1)S(1)}, u32[]{:S(2)}, u32[]{:S(2)}) %collective-permute-start.5) | collective-permute-done | bytes 131104 | tf_op jit(solution)/shard_map/ppermute | solution.py:212
  76.5 0.0 copy-start.4
  76.5 0.0 copy-done.3
  76.5 0.6 copy-done.4
  77.1 5.6 %shard_map.87 = (bf16[8,256,128]{2,1,0:T(8,128)(2,1)}, bf16[8,256,128]{2,1,0:T(8,128)(2,1)}) custom-call(bf16[2,256,128]{2,1,0:T(8,128)(2,1)} %copy-done.3, bf16[8,256,128]{2,1,0:T(8,128)(2,1)} %get-tuple-element.10.mixed_ref, bf16[2,256,128]{2,1,0:T(8,128)(2,1)} %copy-done.4, bf16[3,1152,128]{2,1,0:T(8,128)(2,1)} %bitcast.19, bf16[8,256,128]{2,1,0:T(8,128)(2,1)} %bitcast.29), custom_call_target="tpu_custom_call" | custom-call | flops 1811939328 | bytes 2195456 | tf_op jit(solution)/shard_map/pallas_call | solution.py:198
  82.7 1.0 fusion
  83.7 1.5 collective-permute-start.6
  85.2 1.5 collective-permute-start.7
  86.7 5.0 %shard_map.89 = bf16[3,1152,128]{2,1,0:T(8,128)(2,1)} custom-call(bf16[2,256,128]{2,1,0:T(8,128)(2,1)} %copy-done.3, bf16[8,256,128]{2,1,0:T(8,128)(2,1)} %get-tuple-element.10.mixed_ref, bf16[2,256,128]{2,1,0:T(8,128)(2,1)} %copy-done.4, bf16[8,256,128]{2,1,0:T(8,128)(2,1)} %get-tuple-element.12.grad_ref), custom_call_target="tpu_custom_call" | custom-call | flops 1811939328 | bytes 1310720 | tf_op jit(solution)/shard_map/pallas_call | solution.py:198
  91.7 0.0 collective-permute-done.6.low_ref
  91.7 0.0 copy-start.5
  91.7 0.3 collective-permute-done.7.high_ref
  92.0 0.0 copy-start.6
  92.0 0.3 copy-done.5
  92.4 0.3 copy-done.6
  92.7 16.5 %shard_map.88 = bf16[3,1152,128]{2,1,0:T(8,128)(2,1)} custom-call(bf16[2,256,128]{2,1,0:T(8,128)(2,1)} %copy-done.5, bf16[8,256,128]{2,1,0:T(8,128)(2,1)} %get-tuple-element.12.grad_ref, bf16[2,256,128]{2,1,0:T(8,128)(2,1)} %copy-done.6, bf16[3,1152,128]{2,1,0:T(8,128)(2,1)} %bitcast.20, f32[8,256,128]{2,1,0:T(8,128)} %get-tuple-element.13.slope_own_ref, ...), custom_call_target="tpu_custom_call" | custom-call | flops 5435817984 | bytes 5079040 | tf_op jit(solution)/shard_map/pallas_call | solution.py:198
  109.2 0.0 all-reduce.3.cloned.1.call-update
  109.3 132.9 %all-reduce.3.cloned.1.call-done = (bf16[3,3,3,128,128]{4,3,2,1,0:T(8,128)(2,1)}, bf16[3,3,3,128,128]{4,3,2,1,0:T(8,128)(2,1)}) async-done(((bf16[3,3,3,128,128]{4,3,2,1,0:T(8,128)(2,1)}, bf16[3,3,3,128,128]{4,3,2,1,0:T(8,128)(2,1)}), (bf16[3,3,3,128,128]{4,3,2,1,0:T(8,128)(2,1)}, bf16[3,3,3,128,128]{4,3,2,1,0:T(8,128)(2,1)})) %all-reduce.3.cloned.1.call-update) | async-done | bytes 1769488 | tf_op jit(solution)/shard_map/psum | solution.py:273
  242.2 0.0 copy-start.2
  242.2 2.7 %reshape.59 = f32[3,3,3,128,128]{4,3,2,1,0:T(8,128)} convert(bf16[3,3,3,128,128]{4,3,2,1,0:T(8,128)(2,1)} %get-tuple-element.15) | non-fusion elementwise | flops 442368 | bytes 2654208 | tf_op jit(solution)/shard_map/reshape | solution.py:273
  244.8 0.0 copy-done.2
  244.8 1.4 reshape.61
  (3 shorter events, 0.0 us)
Async XLA Ops:
  7.2 21.8 %all-to-all-start = ((bf16[16,128,128]{2,1,0:T(8,128)(2,1)}), bf16[16,128,128]{2,1,0:T(8,128)(2,1)S(1)}, u32[]{:S(2)}, u32[]{:S(2)}) async-start(bf16[16,128,128]{2,1,0:T(8,128)(2,1)} %bitcast.16), calls=%async_computation | async-start | bytes 1048576 | tf_op jit(solution)/shard_map/all_to_all | solution.py:230
  14.5 20.2 %copy-start = (bf16[1,8,16,16,128]{4,3,2,1,0:T(8,128)(2,1)S(1)}, bf16[1,8,16,16,128]{4,3,2,1,0:T(8,128)(2,1)}, u32[]{:S(2)}) copy-start(bf16[1,8,16,16,128]{4,3,2,1,0:T(8,128)(2,1)} %param.6) | copy-start | bytes 1572868
  14.6 26.1 %copy-start.7 = (f32[16]{0:T(128)S(1)}, f32[16]{0:T(128)}, u32[]{:S(2)}) copy-start(f32[16]{0:T(128)} %param.10) | copy-start | bytes 196
  30.6 18.6 %all-to-all-start.1 = ((bf16[16,128,128]{2,1,0:T(8,128)(2,1)}), bf16[16,128,128]{2,1,0:T(8,128)(2,1)S(1)}, u32[]{:S(2)}, u32[]{:S(2)}) async-start(bf16[16,128,128]{2,1,0:T(8,128)(2,1)} %broadcast_select_fusion), calls=%async_computation.1 | async-start | bytes 1048576 | tf_op jit(solution)/shard_map/all_to_all | solution.py:233
  34.7 207.5 %all-reduce.3.cloned.1.call-start = ((), (), s32[]{:S(2)}) async-start(), calls=%async_computation.2 | async-start | bytes 3538944 | tf_op jit(solution)/shard_map/psum | solution.py:273
  34.8 8.4 %collective-permute-start.3 = (bf16[1,256,128]{2,1,0:T(8,128)(2,1)S(1)}, bf16[1,256,128]{2,1,0:T(8,128)(2,1)S(1)}, u32[]{:S(2)}, u32[]{:S(2)}) collective-permute-start(bf16[1,256,128]{2,1,0:T(8,128)(2,1)S(1)} %bitcast.24), channel_id=1, source_target_pairs={{1,0},{3,2},{5,4},{7,6},{9,8},{11,10},{13,12},{15,14},{17,16},{19,... | collective-permute-start | bytes 196616 | tf_op jit(solution)/shard_map/ppermute | solution.py:212
  36.1 7.1 %collective-permute-start.2 = (bf16[1,256,128]{2,1,0:T(8,128)(2,1)S(1)}, bf16[1,256,128]{2,1,0:T(8,128)(2,1)S(1)}, u32[]{:S(2)}, u32[]{:S(2)}) collective-permute-start(bf16[1,256,128]{2,1,0:T(8,128)(2,1)S(1)} %bitcast.23), channel_id=1, source_target_pairs={{0,1},{2,3},{4,5},{6,7},{8,9},{10,11},{12,13},{14,15},{16,17},{18,... | collective-permute-start | bytes 196616 | tf_op jit(solution)/shard_map/ppermute | solution.py:211
  49.2 11.4 %collective-permute-start.1 = (bf16[1,256,128]{2,1,0:T(8,128)(2,1)S(1)}, bf16[1,256,128]{2,1,0:T(8,128)(2,1)S(1)}, u32[]{:S(2)}, u32[]{:S(2)}) collective-permute-start(bf16[1,256,128]{2,1,0:T(8,128)(2,1)S(1)} %bitcast.26), channel_id=1, source_target_pairs={{1,0},{3,2},{5,4},{7,6},{9,8},{11,10},{13,12},{15,14},{17,16},{19,... | collective-permute-start | bytes 196616 | tf_op jit(solution)/shard_map/ppermute | solution.py:212
  50.5 10.1 %collective-permute-start = (bf16[1,256,128]{2,1,0:T(8,128)(2,1)S(1)}, bf16[1,256,128]{2,1,0:T(8,128)(2,1)S(1)}, u32[]{:S(2)}, u32[]{:S(2)}) collective-permute-start(bf16[1,256,128]{2,1,0:T(8,128)(2,1)S(1)} %bitcast.25), channel_id=1, source_target_pairs={{0,1},{2,3},{4,5},{6,7},{8,9},{10,11},{12,13},{14,15},{16,17},{18,... | collective-permute-start | bytes 196616 | tf_op jit(solution)/shard_map/ppermute | solution.py:211
  61.4 9.5 %copy-start.1 = (bf16[3,3,3,128,128]{4,3,2,1,0:T(8,128)(2,1)S(1)}, bf16[3,3,3,128,128]{4,3,2,1,0:T(8,128)(2,1)}, u32[]{:S(2)}) copy-start(bf16[3,3,3,128,128]{4,3,2,1,0:T(8,128)(2,1)} %param.8) | copy-start | bytes 2654212
  68.3 4.4 %collective-permute-start.4 = (bf16[2,256,128]{2,1,0:T(8,128)(2,1)S(1)}, bf16[2,256,128]{2,1,0:T(8,128)(2,1)S(1)}, u32[]{:S(2)}, u32[]{:S(2)}) collective-permute-start(bf16[2,256,128]{2,1,0:T(8,128)(2,1)S(1)} %get-tuple-element.20), channel_id=1, source_target_pairs={{0,1},{2,3},{4,5},{6,7},{8,9},{10,11},{12,13},{14,15},{16,17},{18,... | collective-permute-start | bytes 393224 | tf_op jit(solution)/shard_map/ppermute | solution.py:211
  69.6 6.9 %collective-permute-start.5 = (bf16[2,256,128]{2,1,0:T(8,128)(2,1)S(1)}, bf16[2,256,128]{2,1,0:T(8,128)(2,1)S(1)}, u32[]{:S(2)}, u32[]{:S(2)}) collective-permute-start(bf16[2,256,128]{2,1,0:T(8,128)(2,1)S(1)} %get-tuple-element.19), channel_id=1, source_target_pairs={{1,0},{3,2},{5,4},{7,6},{9,8},{11,10},{13,12},{15,14},{17,16},{19,... | collective-permute-start | bytes 393224 | tf_op jit(solution)/shard_map/ppermute | solution.py:212
  72.7 3.8 %copy-start.3 = (bf16[2,256,128]{2,1,0:T(8,128)(2,1)}, bf16[2,256,128]{2,1,0:T(8,128)(2,1)S(1)}, u32[]{:S(2)}) copy-start(bf16[2,256,128]{2,1,0:T(8,128)(2,1)S(1)} %collective-permute-done.4.low_ref) | copy-start | bytes 393220
  76.5 0.7 copy-start.4
  83.7 8.0 %collective-permute-start.6 = (bf16[2,256,128]{2,1,0:T(8,128)(2,1)S(1)}, bf16[2,256,128]{2,1,0:T(8,128)(2,1)S(1)}, u32[]{:S(2)}, u32[]{:S(2)}) collective-permute-start(bf16[2,256,128]{2,1,0:T(8,128)(2,1)S(1)} %get-tuple-element.18), channel_id=1, source_target_pairs={{0,1},{2,3},{4,5},{6,7},{8,9},{10,11},{12,13},{14,15},{16,17},{18,... | collective-permute-start | bytes 393224 | tf_op jit(solution)/shard_map/ppermute | solution.py:211
  85.2 6.9 %collective-permute-start.7 = (bf16[2,256,128]{2,1,0:T(8,128)(2,1)S(1)}, bf16[2,256,128]{2,1,0:T(8,128)(2,1)S(1)}, u32[]{:S(2)}, u32[]{:S(2)}) collective-permute-start(bf16[2,256,128]{2,1,0:T(8,128)(2,1)S(1)} %get-tuple-element.17), channel_id=1, source_target_pairs={{1,0},{3,2},{5,4},{7,6},{9,8},{11,10},{13,12},{15,14},{17,16},{19,... | collective-permute-start | bytes 393224 | tf_op jit(solution)/shard_map/ppermute | solution.py:212
  91.7 0.7 copy-start.5
  92.0 0.7 copy-start.6
  242.2 2.7 %copy-start.2 = (bf16[3,3,3,128,128]{4,3,2,1,0:T(8,128)(2,1)S(1)}, bf16[3,3,3,128,128]{4,3,2,1,0:T(8,128)(2,1)}, u32[]{:S(2)}) copy-start(bf16[3,3,3,128,128]{4,3,2,1,0:T(8,128)(2,1)} %get-tuple-element.16) | copy-start | bytes 2654212
Sparse Core Ops, SparseCore 0:
  109.4 132.7 all-reduce.2

commit v2 on v1

--- a/solution.py
+++ b/solution.py
@@ -101,10 +101,21 @@
             yield tap, part[:, place * chans : (place + 1) * chans]
 
 
-def first_kernel_body(width, share_ref, x_ref, kernel_ref, hidden_ref, slope_ref, store, wide_ref):
+def frame_all(store, low_ref, x_ref, high_ref, spread, width):
+    depth = x_ref.shape[0]
+    for layer in range(depth + 2 * spread):
+        if layer < spread:
+            plane = low_ref[layer]
+        elif layer < depth + spread:
+            plane = x_ref[layer - spread]
+        else:
+            plane = high_ref[layer - depth - spread]
+        frame(store, layer, plane, spread, width)
+
+
+def first_kernel_body(width, share_ref, low_ref, x_ref, high_ref, kernel_ref, hidden_ref, slope_ref, store, wide_ref):
     depth, cells, _ = hidden_ref.shape
-    for layer in range(depth + 2):
-        frame(store, layer, x_ref[layer], 1, width)
+    frame_all(store, low_ref, x_ref, high_ref, 1, width)
     fill_pairs(kernel_ref, wide_ref)
     for p, value in conv_pairs(store, wide_ref, depth, 1, width, cells):
         squash = jax.nn.sigmoid(value)
@@ -112,10 +123,9 @@
         slope_ref[p] = share_ref[0] * (squash * (1.0 + value * (1.0 - squash)))
 
 
-def mix_body(width, share_ref, x_ref, kernel_ref, own_ref, mixed_ref, slope_ref, store, wide_ref):
+def mix_body(width, share_ref, low_ref, x_ref, high_ref, kernel_ref, own_ref, mixed_ref, slope_ref, store, wide_ref):
     depth, cells, _ = mixed_ref.shape
-    for layer in range(depth + 2):
-        frame(store, layer, x_ref[layer], 1, width)
+    frame_all(store, low_ref, x_ref, high_ref, 1, width)
     fill_pairs(kernel_ref, wide_ref)
     for p, value in conv_pairs(store, wide_ref, depth, 1, width, cells):
         squash = jax.nn.sigmoid(value)
@@ -126,13 +136,7 @@
 
 def second_body(width, low_ref, mixed_ref, high_ref, kernel_ref, cot_ref, result_ref, grad_ref, store, wide_ref):
     depth, cells, _ = result_ref.shape
-    for layer in range(depth + 4):
-        plane = (
-            low_ref[layer]
-            if layer < 2
-            else (mixed_ref[layer - 2] if layer < depth + 2 else high_ref[layer - depth - 2])
-        )
-        frame(store, layer, plane, 2, width)
+    frame_all(store, low_ref, mixed_ref, high_ref, 2, width)
     fill_pairs(kernel_ref, wide_ref)
     for p, value in conv_pairs(store, wide_ref, depth, 2, width, cells):
         squash = jax.nn.sigmoid(value)
@@ -144,13 +148,7 @@
 
 def second_grad_body(width, low_ref, mixed_ref, high_ref, grad_ref, out_ref, store, total):
     depth, cells, chans = grad_ref.shape
-    for layer in range(depth + 4):
-        plane = (
-            low_ref[layer]
-            if layer < 2
-            else (mixed_ref[layer - 2] if layer < depth + 2 else high_ref[layer - depth - 2])
-        )
-        frame(store, layer, plane, 2, width)
+    frame_all(store, low_ref, mixed_ref, high_ref, 2, width)
 
     def grad_at(p):
         return jnp.zeros((cells, chans), BF16) if p is None else grad_ref[p]
@@ -162,26 +160,19 @@
 
 
 def back_body(
-    width, low_ref, grad_ref, high_ref, kernel_ref, slope_own_ref, slope_mate_ref, own_ref, mate_ref,
-    out_ref, store, wide_ref, term_own, term_mate, store_one, total,
+    width, low_ref, grad_ref, high_ref, kernel_ref, slope_own_ref, slope_mate_ref,
+    own_low, own_ref, own_high, mate_low, mate_ref, mate_high, out_ref, store, wide_ref, term_own, term_mate, store_one, total,
 ):
     depth, cells, chans = grad_ref.shape
-    for layer in range(depth + 4):
-        plane = (
-            low_ref[layer]
-            if layer < 2
-            else (grad_ref[layer - 2] if layer < depth + 2 else high_ref[layer - depth - 2])
-        )
-        frame(store, layer, plane, 2, width)
+    frame_all(store, low_ref, grad_ref, high_ref, 2, width)
     fill_pairs(kernel_ref, wide_ref)
     for p, value in conv_pairs(store, wide_ref, depth, 2, width, cells):
         value = value.astype(BF16).astype(F32)
         term_own[p] = (value * slope_own_ref[p]).astype(BF16)
         term_mate[p] = (value * slope_mate_ref[p]).astype(BF16)
     total[...] = jnp.zeros_like(total)
-    for x_ref, term in ((own_ref, term_own), (mate_ref, term_mate)):
-        for layer in range(depth + 2):
-            frame(store_one, layer, x_ref[layer], 1, width)
+    for faces, term in (((own_low, own_ref, own_high), term_own), ((mate_low, mate_ref, mate_high), term_mate)):
+        frame_all(store_one, *faces, 1, width)
 
         def grad_at(p, term=term):
             return jnp.zeros((cells, chans), BF16) if p is None else term[p]
@@ -206,6 +197,243 @@
     )(*args)
 
 
+def neighbours(count):
+    me = lax.axis_index("space")
+    return (me > 0, {"space": me - 1}), (me < count - 1, {"space": me + 1})
+
+
+def greet(peers, ends):
+    barrier = pltpu.get_barrier_semaphore()
+    for peer in peers:
+        pl.semaphore_signal(barrier, inc=1, device_id=peer, device_id_type=pl.DeviceIdType.MESH)
+    for exists, peer in ends:
+
+        @pl.when(exists)
+        def _(peer=peer):
+            pl.semaphore_signal(barrier, inc=1, device_id=peer, device_id_type=pl.DeviceIdType.MESH)
+
+    waits = len(peers)
+    if ends:
+        me = lax.axis_index("space")
+        waits = waits + jnp.minimum(me, 1) + jnp.minimum(lax.axis_size("space") - 1 - me, 1)
+    pl.semaphore_wait(barrier, waits)
+
+
+class Faces:
+    def __init__(self, ends, head, tail, low, high, send, recv):
+        (self.below, down), (self.above, up) = ends
+        self.low, self.high = low, high
+        self.down = pltpu.make_async_remote_copy(
+            src_ref=head, dst_ref=high, send_sem=send.at[0], recv_sem=recv.at[0],
+            device_id=down, device_id_type=pl.DeviceIdType.MESH,
+        )
+        self.up = pltpu.make_async_remote_copy(
+            src_ref=tail, dst_ref=low, send_sem=send.at[1], recv_sem=recv.at[1],
+            device_id=up, device_id_type=pl.DeviceIdType.MESH,
+        )
+
+    def start(self):
+        pl.when(self.below)(self.down.start)
+        pl.when(self.above)(self.up.start)
+
+    def finish(self):
+        @pl.when(self.below)
+        def _():
+            self.down.wait_send()
+            self.up.wait_recv()
+
+        @pl.when(jnp.logical_not(self.below))
+        def _():
+            self.low[...] = jnp.zeros(self.low.shape, self.low.dtype)
+
+        @pl.when(self.above)
+        def _():
+            self.up.wait_send()
+            self.down.wait_recv()
+
+        @pl.when(jnp.logical_not(self.above))
+        def _():
+            self.high[...] = jnp.zeros(self.high.shape, self.high.dtype)
+
+
+def exchange_body(
+    count, slabs, partner_ref, x_ref, mate_ref, low_ref, high_ref, mate_low_ref, mate_high_ref,
+    got_a, got_b, stage, send_one, recv_one, send_two, recv_two, send_face, recv_face,
+):
+    me = lax.axis_index("sample")
+    peers = [lax.rem(me + step, count) for step in range(1, count)]
+    ends = neighbours(slabs)
+    greet([{"sample": peer} for peer in peers], ends)
+    got = (got_a, got_b)
+    rows = got_a.shape[1]
+    layer = low_ref.shape[0]
+
+    def faces(cells, low, high, kind):
+        return Faces(
+            ends, cells.at[pl.ds(0, layer)], cells.at[pl.ds(count - layer, layer)], low, high,
+            send_face.at[kind], recv_face.at[kind],
+        )
+
+    def push(src, dst, send, recv, peer):
+        return pltpu.make_async_remote_copy(
+            src_ref=src, dst_ref=dst, send_sem=send, recv_sem=recv,
+            device_id={"sample": peer}, device_id_type=pl.DeviceIdType.MESH,
+        )
+
+    first, second = [], []
+    for part in range(2):
+        span = pl.ds(part * rows, rows)
+        first.append([
+            push(x_ref.at[peer, span], got[part].at[me], send_one.at[part, place], recv_one.at[part, place], peer)
+            for place, peer in enumerate(peers)
+        ])
+        for copy in first[part]:
+            copy.start()
+    own = faces(x_ref, low_ref, high_ref, 0)
+    own.start()
+    for part in range(2):
+        span = pl.ds(part * rows, rows)
+        got[part][me] = x_ref[me, span]
+        for copy in first[part]:
+            copy.wait_recv()
+        second.append([])
+        for place, peer in enumerate(peers):
+            stage[part, place] = got[part][partner_ref[peer]]
+            copy = push(
+                stage.at[part, place], mate_ref.at[me, span],
+                send_two.at[part, place], recv_two.at[part, place], peer,
+            )
+            copy.start()
+            second[part].append(copy)
+        mate_ref[me, span] = got[part][partner_ref[me]]
+    for copies in second:
+        for copy in copies:
+            copy.wait_recv()
+    mates = faces(mate_ref, mate_low_ref, mate_high_ref, 1)
+    mates.start()
+    for copies in first + second:
+        for copy in copies:
+            copy.wait_send()
+    own.finish()
+    mates.finish()
+
+
+def exchange(x, partner, count, slabs):
+    depth, cells, chans = x.shape
+    piece = depth * cells // count
+    layer = cells // piece
+    rows = piece // 2
+    dma = pltpu.SemaphoreType.DMA
+    vmem = pl.BlockSpec(memory_space=pltpu.VMEM)
+    edge = jax.ShapeDtypeStruct((layer, piece, chans), BF16)
+    mate, *rest = pl.pallas_call(
+        functools.partial(exchange_body, count, slabs),
+        out_shape=[jax.ShapeDtypeStruct((count, piece, chans), BF16)] + [edge] * 4,
+        in_specs=[pl.BlockSpec(memory_space=pltpu.SMEM), vmem],
+        out_specs=[vmem] * 5,
+        scratch_shapes=[
+            pltpu.VMEM((count, rows, chans), BF16),
+            pltpu.VMEM((count, rows, chans), BF16),
+            pltpu.VMEM((2, count - 1, rows, chans), BF16),
+            dma((2, count - 1)), dma((2, count - 1)), dma((2, count - 1)), dma((2, count - 1)),
+            dma((2, 2)), dma((2, 2)),
+        ],
+        compiler_params=pltpu.CompilerParams(
+            collective_id=0, has_side_effects=True, vmem_limit_bytes=VMEM_LIMIT
+        ),
+    )(partner, x.reshape(count, piece, chans))
+    return [mate.reshape(depth, cells, chans)] + [a.reshape(1, cells, chans) for a in rest]
+
+
+class Total:
+    def __init__(self, order, held, landing, full, send, recv):
+        self.held, self.landing, self.full, self.send, self.recv = held, landing, full, send, recv
+        start, size, base = 0, held.shape[0], 0
+        self.plan = []
+        for axis, bit in order:
+            me = lax.axis_index(axis)
+            half = size // 2
+            mine = lax.rem(me // (1 << bit), 2)
+            peer = {axis: me + (1 - 2 * mine) * (1 << bit)}
+            keep = start + mine * half
+            self.plan.append((peer, keep, start + (1 - mine) * half, half, base))
+            start, size, base = keep, half, base + half
+        self.copy = None
+
+    def rows(self, start, size):
+        return pl.ds(pl.multiple_of(start, 16), size)
+
+    def begin(self, turn):
+        count = len(self.plan)
+        if turn < count:
+            peer, _, away, half, base = self.plan[turn]
+            src = self.held.at[self.rows(away, half)]
+            dst = self.landing.at[pl.ds(base, half)]
+        else:
+            peer, keep, _, half, _ = self.plan[2 * count - 1 - turn]
+            if turn == count:
+                self.full[self.rows(keep, half)] = self.held[self.rows(keep, half)]
+            src = dst = self.full.at[self.rows(keep, half)]
+        self.copy = pltpu.make_async_remote_copy(
+            src_ref=src, dst_ref=dst, send_sem=self.send.at[turn], recv_sem=self.recv.at[turn],
+            device_id=peer, device_id_type=pl.DeviceIdType.MESH,
+        )
+        self.copy.start()
+
+    def end(self, turn):
+        self.copy.wait()
+        if turn < len(self.plan):
+            _, keep, _, half, base = self.plan[turn]
+            span = self.rows(keep, half)
+            self.held[span] = (
+                self.held[span].astype(F32) + self.landing[pl.ds(base, half)].astype(F32)
+            ).astype(BF16)
+
+
+def sum_orders(count, slabs):
+    samples = [("sample", bit) for bit in range(count.bit_length() - 1)]
+    spaces = [("space", bit) for bit in range(slabs.bit_length() - 1)]
+    return samples[:2] + spaces + samples[2:], samples[:1] + spaces + samples[1:]
+
+
+def totals_body(count, slabs, one_ref, two_ref, full_one, full_two, held_one, held_two, land_one, land_two, send, recv):
+    orders = sum_orders(count, slabs)
+    peers = []
+    for axis, bit in orders[0]:
+        me = lax.axis_index(axis)
+        peers.append({axis: me + (1 - 2 * lax.rem(me // (1 << bit), 2)) * (1 << bit)})
+    greet(peers, ())
+    held_one[...] = one_ref[...]
+    held_two[...] = two_ref[...]
+    sums = [
+        Total(orders[0], held_one, land_one, full_one, send.at[0], recv.at[0]),
+        Total(orders[1], held_two, land_two, full_two, send.at[1], recv.at[1]),
+    ]
+    for turn in range(2 * len(orders[0])):
+        for item in sums:
+            item.begin(turn)
+        for item in sums:
+            item.end(turn)
+
+
+def totals(one, two, count, slabs):
+    rows, chans = one.shape
+    vmem = pl.BlockSpec(memory_space=pltpu.VMEM)
+    buffer = pltpu.VMEM((rows, chans), BF16)
+    turns = 2 * len(sum_orders(count, slabs)[0])
+    return pl.pallas_call(
+        functools.partial(totals_body, count, slabs),
+        out_shape=[jax.ShapeDtypeStruct((rows, chans), BF16)] * 2,
+        in_specs=[vmem] * 2,
+        out_specs=[vmem] * 2,
+        scratch_shapes=[buffer] * 4
+        + [pltpu.SemaphoreType.DMA((2, turns)), pltpu.SemaphoreType.DMA((2, turns))],
+        compiler_params=pltpu.CompilerParams(
+            collective_id=1, has_side_effects=True, vmem_limit_bytes=VMEM_LIMIT
+        ),
+    )(one, two)
+
+
 def edges(block, width):
     count = lax.axis_size("space")
     low = lax.ppermute(block[-width:], "space", [(i, i + 1) for i in range(count - 1)])
@@ -226,17 +454,9 @@
     flipped = jnp.transpose(jnp.flip(second_kernel, (0, 1, 2)), (0, 1, 2, 4, 3)).reshape(
         3, 9 * chans, chans
     )
-    count = lax.axis_size("sample")
-    pieces = lax.all_to_all(
-        x.reshape(count, depth * cells // count, chans), "sample", split_axis=0, concat_axis=0, tiled=True
-    )
-    mate = lax.all_to_all(
-        jnp.take(pieces, partner, axis=0), "sample", split_axis=0, concat_axis=0, tiled=True
-    ).reshape(depth, cells, chans)
-    low, high = edges(x, 1)
-    own_pad = jnp.concatenate([low, x, high], axis=0)
-    low, high = edges(mate, 1)
-    mate_pad = jnp.concatenate([low, mate, high], axis=0)
+    count, slabs = lax.axis_size("sample"), lax.axis_size("space")
+    mate, low, high, mate_low, mate_high = exchange(x, partner, count, slabs)
+    own_pad, mate_pad = (low, x, high), (mate_low, mate, mate_high)
     layer = (depth, cells, chans)
     half = jax.ShapeDtypeStruct(layer, BF16)
     full = jax.ShapeDtypeStruct(layer, F32)
@@ -246,10 +466,10 @@
     wide = pltpu.VMEM((4, 9 * chans, 2 * chans), BF16)
     total = pltpu.VMEM((3, 9 * chans, chans), F32)
     hidden, slope_own = call(
-        first_kernel_body, width, (shares, own_pad, flat_one), (half, full), [store_one, wide], unit, 1
+        first_kernel_body, width, (shares, *own_pad, flat_one), (half, full), [store_one, wide], unit, 1
     )
     mixed, slope_mate = call(
-        mix_body, width, (shares, mate_pad, flat_one, hidden), (half, full), [store_one, wide], unit, 1
+        mix_body, width, (shares, *mate_pad, flat_one, hidden), (half, full), [store_one, wide], unit, 1
     )
     low, high = edges(mixed, 2)
     result, grad_two = call(
@@ -263,14 +483,22 @@
     first_local = call(
         back_body,
         width,
-        (low, grad_two, high, flipped, slope_own, slope_mate, own_pad, mate_pad),
+        (low, grad_two, high, flipped, slope_own, slope_mate, *own_pad, *mate_pad),
         terms,
         [store_two, wide, pltpu.VMEM(layer, BF16), pltpu.VMEM(layer, BF16), store_one, total],
         3 * unit,
     )
     shape = first_kernel.shape
-    second_sum = lax.psum(second_local, ("sample", "space")).astype(F32).reshape(shape)
-    first_sum = lax.psum(first_local, ("sample", "space")).astype(F32).reshape(shape)
+    rows = 27 * chans
+    unit_rows = 16 * count * slabs
+    spare = -rows % unit_rows
+    second_sum, first_sum = totals(
+        *[jnp.pad(a.reshape(rows, chans), ((0, spare), (0, 0))) for a in (second_local, first_local)],
+        count,
+        slabs,
+    )
+    second_sum = second_sum[:rows].astype(F32).reshape(shape)
+    first_sum = first_sum[:rows].astype(F32).reshape(shape)
     return result.reshape(volume.shape), first_sum, second_sum
 
 

time: 254 us -> 151 us (0.59)
  waiting for transfers between devices: 155 us -> 3.77 us
  Pallas kernels: 38.5 us -> 123 us
  starting transfers between devices: 28.7 us -> 6.64 us
  between operations: 14.9 us -> 1.39 us
  local copies, waits for them, and re-layouts: 6.3 us -> 11.9 us
  other arithmetic: 9.5 us -> 4.12 us
    psum x1 -> x0, waiting for transfers between devices: 133 us -> none  [shards(): lax.psum(first_local, ('sample', 'space')).astype(F32).reshape(shape)]
    pallas_call x0 -> x2, Pallas kernels: none -> 84.1 us  [the longest x1 49.2 us: totals(): pl.pallas_call(functools.partial(totals_body, count, slabs), out_shape=[j...]
    all_to_all x2 -> x0, waiting for transfers between devices: 18.1 us -> none  [the longest x1 13.1 us: shards(): lax.all_to_all(x.reshape(count, depth * cells // count, chans), 'sample',...]
    all_to_all x2 -> x0, starting transfers between devices: 11.5 us -> none  [the longest x1 7.37 us: shards(): lax.all_to_all(x.reshape(count, depth * cells // count, chans), 'sample',...]
    ppermute x4 -> x2, starting transfers between devices: 11.9 us -> 3.88 us  [edges(): lax.ppermute(block[-width:], 'space', [(i, i + 1) for i in range(count -...]
    pad x0 -> x2, local copies, waits for them, and re-layouts: none -> 4.3 us  [shards(): jnp.pad(a.reshape(rows, chans), ((0, spare), (0, 0)))]
    ppermute x4 -> x2, starting transfers between devices: 5.35 us -> 2.76 us  [edges(): lax.ppermute(block[:width], 'space', [(i + 1, i) for i in range(count - 1)])]
  transfers between devices with their start and end apart: 11 -> 4, of which waited for: 5 -> 1; matrix products, arithmetic and copies ran while one was open for 2% -> 3% of each run, Pallas kernels for 4% -> 3%
where the time goes in v2:
time: 151 us; the launch traced here: 150 us
  Pallas kernels  123 us (81%)
  local copies, waits for them, and re-layouts  11.9 us (8%)
  starting transfers between devices  6.64 us (4%)
  other arithmetic  4.12 us (3%)
  waiting for transfers between devices  3.77 us (2%)
    pallas_call x1, Pallas kernels, totals(): pl.pallas_call(functools.partial(totals_body, count, slabs), out_shape=[j...  49.2 us
    pallas_call x5, Pallas kernels, call(): pl.pallas_call(functools.partial(body, width), out_shape=outs, in_specs=[...  38.5 us
    pallas_call x1, Pallas kernels, exchange(): pl.pallas_call(functools.partial(exchange_body, count, slabs), out_shape=...  34.9 us
    pad x2, local copies, waits for them, and re-layouts, shards(): jnp.pad(a.reshape(rows, chans), ((0, spare), (0, 0)))  4.3 us
    ppermute x2, starting transfers between devices, edges(): lax.ppermute(block[-width:], 'space', [(i, i + 1) for i in range(count -...  3.88 us
    ppermute x2, waiting for transfers between devices, edges(): lax.ppermute(block[:width], 'space', [(i + 1, i) for i in range(count - 1)])  3.77 us
  transfers between devices with their start and end apart: 4, of which 1 were waited for; matrix products, arithmetic and copies ran while one was open for 3% of the time, Pallas kernels for 3%

profile of v2, /device:TPU:0, one launch (start us, length us, event | category | flops | bytes accessed | tf_op | source)
XLA Modules:
  0.0 150.5 jit_solution(12350867323490394505)
XLA Ops:
  0.6 1.2 dynamic_slice.3
  2.5 1.3 pad_maximum_fusion.share_ref
  3.8 34.9 %shard_map.85 = (bf16[16,128,128]{2,1,0:T(8,128)(2,1)}, bf16[2,128,128]{2,1,0:T(8,128)(2,1)}, bf16[2,128,128]{2,1,0:T(8,128)(2,1)}, bf16[2,128,128]{2,1,0:T(8,128)(2,1)}, bf16[2,128,128]{2,1,0:T(8,128)(2,1)}) custom-call(s32[16]{0:T(128)} %partner_ref.1, bf16[16,128,128]{2,1,0:T(8,128)(2,1)} %bitcast.26), custom_call_target="tpu_custom_call" | custom-call | tf_op jit(solution)/shard_map/pallas_call | solution.py:329
  38.8 5.5 %shard_map.86 = (bf16[8,256,128]{2,1,0:T(8,128)(2,1)}, f32[8,256,128]{2,1,0:T(8,128)}) custom-call(f32[2]{0:T(128)} %pad_maximum_fusion.share_ref, bf16[1,256,128]{2,1,0:T(8,128)(2,1)} %bitcast.34, bf16[8,256,128]{2,1,0:T(8,128)(2,1)} %bitcast.27, bf16[1,256,128]{2,1,0:T(8,128)(2,1)} %bitcast.36, bf16[3,1152,128]{2,1,0:T(8,128)(2,1)} %bitcast.29), custom_call_target="tpu_custom_call" | custom-call | flops 1811939328 | bytes 1540104 | tf_op jit(solution)/shard_map/pallas_call | solution.py:189
  44.3 0.0 copy-start
  44.3 5.9 %shard_map.87 = (bf16[8,256,128]{2,1,0:T(8,128)(2,1)}, f32[8,256,128]{2,1,0:T(8,128)}) custom-call(f32[2]{0:T(128)} %pad_maximum_fusion.share_ref, bf16[1,256,128]{2,1,0:T(8,128)(2,1)} %bitcast.38, bf16[8,256,128]{2,1,0:T(8,128)(2,1)} %bitcast.32, bf16[1,256,128]{2,1,0:T(8,128)(2,1)} %bitcast.40, bf16[3,1152,128]{2,1,0:T(8,128)(2,1)} %bitcast.30, ...), custom_call_target="tpu_custom_call" | custom-call | flops 1811939328 | bytes 2064392 | tf_op jit(solution)/shard_map/pallas_call | solution.py:189
  50.1 1.0 fusion.1
  51.1 2.4 %collective-permute-start = (bf16[2,256,128]{2,1,0:T(8,128)(2,1)S(1)}, bf16[2,256,128]{2,1,0:T(8,128)(2,1)S(1)}, u32[]{:S(2)}, u32[]{:S(2)}) collective-permute-start(bf16[2,256,128]{2,1,0:T(8,128)(2,1)S(1)} %get-tuple-element.32), channel_id=1, source_target_pairs={{0,1},{2,3},{4,5},{6,7},{8,9},{10,11},{12,13},{14,15},{16,17},{18,... | collective-permute-start | bytes 393224 | tf_op jit(solution)/shard_map/ppermute | solution.py:439
  53.5 1.3 collective-permute-start.1
  54.8 0.0 copy-done
  54.8 0.1 reverse_bitcast_fusion
  54.9 1.7 %copy.9 = bf16[3,3,3,128,128]{4,3,2,1,0:T(8,128)(2,1)} copy(bf16[3,3,3,128,128]{3,4,2,1,0:T(8,128)(2,1)S(1)} %reverse_bitcast_fusion) | data formatting | bytes 1769472 | tf_op jit(solution)/shard_map/transpose | solution.py:454
  56.6 0.0 collective-permute-done.low_ref
  56.6 0.0 copy-start.2
  56.6 3.8 %collective-permute-done.1.high_ref = bf16[2,256,128]{2,1,0:T(8,128)(2,1)S(1)} collective-permute-done((bf16[2,256,128]{2,1,0:T(8,128)(2,1)S(1)}, bf16[2,256,128]{2,1,0:T(8,128)(2,1)S(1)}, u32[]{:S(2)}, u32[]{:S(2)}) %collective-permute-start.1) | collective-permute-done | bytes 131104 | tf_op jit(solution)/shard_map/ppermute | solution.py:440
  60.4 0.0 copy-start.4
  60.4 0.0 copy-done.2
  60.4 0.7 copy-done.4
  61.0 5.6 %shard_map.88 = (bf16[8,256,128]{2,1,0:T(8,128)(2,1)}, bf16[8,256,128]{2,1,0:T(8,128)(2,1)}) custom-call(bf16[2,256,128]{2,1,0:T(8,128)(2,1)} %copy-done.2, bf16[8,256,128]{2,1,0:T(8,128)(2,1)} %get-tuple-element.22.mixed_ref, bf16[2,256,128]{2,1,0:T(8,128)(2,1)} %copy-done.4, bf16[3,1152,128]{2,1,0:T(8,128)(2,1)} %bitcast.22, bf16[8,256,128]{2,1,0:T(8,128)(2,1)} %bitcast.31), custom_call_target="tpu_custom_call" | custom-call | flops 1811939328 | bytes 2195456 | tf_op jit(solution)/shard_map/pallas_call | solution.py:189
  66.6 1.0 fusion
  67.6 1.5 collective-permute-start.2
  69.1 1.5 collective-permute-start.3
  70.6 5.1 %shard_map.89 = bf16[3,1152,128]{2,1,0:T(8,128)(2,1)} custom-call(bf16[2,256,128]{2,1,0:T(8,128)(2,1)} %copy-done.2, bf16[8,256,128]{2,1,0:T(8,128)(2,1)} %get-tuple-element.22.mixed_ref, bf16[2,256,128]{2,1,0:T(8,128)(2,1)} %copy-done.4, bf16[8,256,128]{2,1,0:T(8,128)(2,1)} %get-tuple-element.24.grad_ref), custom_call_target="tpu_custom_call" | custom-call | flops 1811939328 | bytes 1310720 | tf_op jit(solution)/shard_map/pallas_call | solution.py:189
  75.6 2.1 %pad.7.one_ref = bf16[3584,128]{1,0:T(8,128)(2,1)} pad(bf16[3456,128]{1,0:T(8,128)(2,1)} %bitcast.25, bf16[]{:T(256)} %constant.14.clone.1), padding=0_128x0_0 | pad | bytes 1802242 | tf_op jit(solution)/shard_map/jit(_pad)/pad | solution.py:496
  77.8 0.0 collective-permute-done.2.low_ref
  77.8 0.0 copy-start.3
  77.8 0.0 collective-permute-done.3.high_ref
  77.8 0.0 copy-start.5
  77.8 0.7 copy-done.3
  78.5 0.0 copy-done.5
  78.5 16.5 %shard_map.90 = bf16[3,1152,128]{2,1,0:T(8,128)(2,1)} custom-call(bf16[2,256,128]{2,1,0:T(8,128)(2,1)} %copy-done.3, bf16[8,256,128]{2,1,0:T(8,128)(2,1)} %get-tuple-element.24.grad_ref, bf16[2,256,128]{2,1,0:T(8,128)(2,1)} %copy-done.5, bf16[3,1152,128]{2,1,0:T(8,128)(2,1)} %bitcast.23, f32[8,256,128]{2,1,0:T(8,128)} %get-tuple-element.25.slope_own_ref, ...), custom_call_target="tpu_custom_call" | custom-call | flops 5435817984 | bytes 5079040 | tf_op jit(solution)/shard_map/pallas_call | solution.py:189
  95.0 2.2 %pad.8.two_ref = bf16[3584,128]{1,0:T(8,128)(2,1)} pad(bf16[3456,128]{1,0:T(8,128)(2,1)} %bitcast.24, bf16[]{:T(256)} %constant.14.clone.1), padding=0_128x0_0 | pad | bytes 1802242 | tf_op jit(solution)/shard_map/jit(_pad)/pad | solution.py:496
  97.2 49.2 %shard_map.91 = (bf16[3584,128]{1,0:T(8,128)(2,1)}, bf16[3584,128]{1,0:T(8,128)(2,1)}) custom-call(bf16[3584,128]{1,0:T(8,128)(2,1)} %pad.7.one_ref, bf16[3584,128]{1,0:T(8,128)(2,1)} %pad.8.two_ref), custom_call_target="tpu_custom_call" | custom-call | tf_op jit(solution)/shard_map/pallas_call | solution.py:424
  146.4 1.2 slice.22
  147.6 0.0 copy-start.1
  147.6 1.4 convert.2
  149.0 0.0 copy-done.1
  149.0 0.1 slice.23
  149.1 1.4 convert.3
Async XLA Ops:
  44.3 10.6 %copy-start = (bf16[3,3,3,128,128]{4,3,2,1,0:T(8,128)(2,1)S(1)}, bf16[3,3,3,128,128]{4,3,2,1,0:T(8,128)(2,1)}, u32[]{:S(2)}) copy-start(bf16[3,3,3,128,128]{4,3,2,1,0:T(8,128)(2,1)} %param.8) | copy-start | bytes 2654212
  51.1 5.5 %collective-permute-start = (bf16[2,256,128]{2,1,0:T(8,128)(2,1)S(1)}, bf16[2,256,128]{2,1,0:T(8,128)(2,1)S(1)}, u32[]{:S(2)}, u32[]{:S(2)}) collective-permute-start(bf16[2,256,128]{2,1,0:T(8,128)(2,1)S(1)} %get-tuple-element.32), channel_id=1, source_target_pairs={{0,1},{2,3},{4,5},{6,7},{8,9},{10,11},{12,13},{14,15},{16,17},{18,... | collective-permute-start | bytes 393224 | tf_op jit(solution)/shard_map/ppermute | solution.py:439
  53.5 6.9 %collective-permute-start.1 = (bf16[2,256,128]{2,1,0:T(8,128)(2,1)S(1)}, bf16[2,256,128]{2,1,0:T(8,128)(2,1)S(1)}, u32[]{:S(2)}, u32[]{:S(2)}) collective-permute-start(bf16[2,256,128]{2,1,0:T(8,128)(2,1)S(1)} %get-tuple-element.31), channel_id=1, source_target_pairs={{1,0},{3,2},{5,4},{7,6},{9,8},{11,10},{13,12},{15,14},{17,16},{19,... | collective-permute-start | bytes 393224 | tf_op jit(solution)/shard_map/ppermute | solution.py:440
  56.6 3.8 %copy-start.2 = (bf16[2,256,128]{2,1,0:T(8,128)(2,1)}, bf16[2,256,128]{2,1,0:T(8,128)(2,1)S(1)}, u32[]{:S(2)}) copy-start(bf16[2,256,128]{2,1,0:T(8,128)(2,1)S(1)} %collective-permute-done.low_ref) | copy-start | bytes 393220
  60.4 0.7 copy-start.4
  67.6 10.2 %collective-permute-start.2 = (bf16[2,256,128]{2,1,0:T(8,128)(2,1)S(1)}, bf16[2,256,128]{2,1,0:T(8,128)(2,1)S(1)}, u32[]{:S(2)}, u32[]{:S(2)}) collective-permute-start(bf16[2,256,128]{2,1,0:T(8,128)(2,1)S(1)} %get-tuple-element.30), channel_id=1, source_target_pairs={{0,1},{2,3},{4,5},{6,7},{8,9},{10,11},{12,13},{14,15},{16,17},{18,... | collective-permute-start | bytes 393224 | tf_op jit(solution)/shard_map/ppermute | solution.py:439
  69.1 8.7 %collective-permute-start.3 = (bf16[2,256,128]{2,1,0:T(8,128)(2,1)S(1)}, bf16[2,256,128]{2,1,0:T(8,128)(2,1)S(1)}, u32[]{:S(2)}, u32[]{:S(2)}) collective-permute-start(bf16[2,256,128]{2,1,0:T(8,128)(2,1)S(1)} %get-tuple-element.29), channel_id=1, source_target_pairs={{1,0},{3,2},{5,4},{7,6},{9,8},{11,10},{13,12},{15,14},{17,16},{19,... | collective-permute-start | bytes 393224 | tf_op jit(solution)/shard_map/ppermute | solution.py:440
  77.8 0.7 copy-start.3
  77.8 0.7 copy-start.5
  147.6 1.4 copy-start.1

commit v3 on v2

v3 whole, which is shorter than its diff:
```python
import functools

import jax
import jax.numpy as jnp
from jax import lax
from jax.experimental import pallas as pl
from jax.experimental.pallas import tpu as pltpu
from jax.sharding import PartitionSpec as P

F32 = jnp.float32
BF16 = jnp.bfloat16
VMEM_LIMIT = 56 * 1024 * 1024


def slope(value):
    squash = jax.nn.sigmoid(value)
    return squash * (1.0 + value * (1.0 - squash))


def groups(depth, spread):
    first = [p for p in range(depth) if (p // spread) % 2 == 0]
    return first, [p + spread for p in first]


def frame(store, layer, plane, spread, width):
    cells, chans = plane.shape
    edge = spread * width
    wide = plane.astype(F32)
    column = lax.broadcasted_iota(jnp.int32, plane.shape, 0) % width
    left = jnp.where(column >= spread, pltpu.roll(wide, spread, 0), 0.0).astype(BF16)
    right = jnp.where(column < width - spread, pltpu.roll(wide, cells - spread, 0), 0.0).astype(BF16)
    store[layer, pl.ds(0, edge), :] = jnp.zeros((edge, 3 * chans), BF16)
    store[layer, pl.ds(edge + cells, edge), :] = jnp.zeros((edge, 3 * chans), BF16)
    for place, value in enumerate((left, plane, right)):
        store[layer, pl.ds(edge, cells), pl.ds(place * chans, chans)] = value


def taps(store, layer, spread, width, cells):
    return jnp.concatenate(
        [store[layer, pl.ds(row * spread * width, cells), :] for row in range(3)], axis=1
    )


def fill_pairs(kernel_ref, wide_ref):
    chans = kernel_ref.shape[2]
    for step in range(4):
        for out in range(2):
            depth_tap = step - out
            block = (
                kernel_ref[depth_tap]
                if 0 <= depth_tap < 3
                else jnp.zeros(kernel_ref.shape[1:], BF16)
            )
            wide_ref[step, :, pl.ds(out * chans, chans)] = block


def fill_back(kernel_ref, wide_ref):
    chans = kernel_ref.shape[2]
    for step in range(4):
        for out in range(2):
            depth_tap = step - out
            for place in range(9):
                block = (
                    kernel_ref[2 - depth_tap, pl.ds((8 - place) * chans, chans)]
                    if 0 <= depth_tap < 3
                    else jnp.zeros((chans, chans), BF16)
                )
                wide_ref[step, pl.ds(out * chans, chans), pl.ds(place * chans, chans)] = block


def conv_pairs(store, wide_ref, depth, spread, width, cells, back=False):
    first, _ = groups(depth, spread)
    side = 1 if back else 0
    total = None
    for half in range(2):
        rows = []
        for p in first:
            rows.append(
                jnp.concatenate(
                    [
                        taps(store, p + spread * (2 * half + k), spread, width, cells)
                        for k in range(2)
                    ],
                    axis=1,
                )
            )
        lhs = jnp.concatenate(rows, axis=0)
        rhs = jnp.concatenate([wide_ref[2 * half], wide_ref[2 * half + 1]], axis=side)
        part = lax.dot_general(lhs, rhs, (((1,), (side,)), ((), ())), preferred_element_type=F32)
        total = part if total is None else total + part
    chans = total.shape[1] // 2
    for place, p in enumerate(first):
        for out in range(2):
            yield p + out * spread, total[
                place * cells : (place + 1) * cells, out * chans : (out + 1) * chans
            ]


def grad_blocks(store, grad_at, depth, spread, width, cells):
    ranges = ((0, 2 * spread, (0, 1)), (2 * spread, depth, (0, 1, 2)), (depth, depth + 2 * spread, (1, 2)))
    for low, high, depth_taps in ranges:
        lhs = jnp.concatenate(
            [taps(store, e, spread, width, cells) for e in range(low, high)], axis=0
        )
        columns = []
        for tap in depth_taps:
            layers = []
            for e in range(low, high):
                p = e - spread * tap
                layers.append(grad_at(p if 0 <= p < depth else None))
            columns.append(jnp.concatenate(layers, axis=0))
        rhs = jnp.concatenate(columns, axis=1)
        part = lax.dot_general(lhs, rhs, (((0,), (0,)), ((), ())), preferred_element_type=F32)
        chans = columns[0].shape[1]
        for place, tap in enumerate(depth_taps):
            yield tap, part[:, place * chans : (place + 1) * chans]


def frame_all(store, low_ref, x_ref, high_ref, spread, width, layers=None):
    depth = x_ref.shape[0]
    for layer in range(depth + 2 * spread) if layers is None else layers:
        if layer < spread:
            plane = low_ref[layer]
        elif layer < depth + spread:
            plane = x_ref[layer - spread]
        else:
            plane = high_ref[layer - depth - spread]
        frame(store, layer, plane, spread, width)


def second_body(width, low_ref, mixed_ref, high_ref, kernel_ref, cot_ref, result_ref, grad_ref, store, wide_ref):
    depth, cells, _ = result_ref.shape
    frame_all(store, low_ref, mixed_ref, high_ref, 2, width)
    fill_pairs(kernel_ref, wide_ref)
    for p, value in conv_pairs(store, wide_ref, depth, 2, width, cells):
        squash = jax.nn.sigmoid(value)
        result_ref[p] = (value * squash).astype(BF16)
        grad_ref[p] = (
            cot_ref[p].astype(F32) * (squash * (1.0 + value * (1.0 - squash)))
        ).astype(BF16)


def call(body, width, args, outs, scratch, flops, smem=0):
    vmem = pl.BlockSpec(memory_space=pltpu.VMEM)
    scalar = pl.BlockSpec(memory_space=pltpu.SMEM)
    size = sum(a.size * a.dtype.itemsize for a in args)
    return pl.pallas_call(
        functools.partial(body, width),
        out_shape=outs,
        in_specs=[scalar] * smem + [vmem] * (len(args) - smem),
        out_specs=jax.tree.map(lambda _: vmem, outs),
        scratch_shapes=scratch,
        compiler_params=pltpu.CompilerParams(vmem_limit_bytes=VMEM_LIMIT),
        cost_estimate=pl.CostEstimate(flops=flops, bytes_accessed=size, transcendentals=0),
    )(*args)


def neighbours(count):
    me = lax.axis_index("space")
    return (me > 0, {"space": me - 1}), (me < count - 1, {"space": me + 1})


def greet(peers, ends):
    barrier = pltpu.get_barrier_semaphore()
    for peer in peers:
        pl.semaphore_signal(barrier, inc=1, device_id=peer, device_id_type=pl.DeviceIdType.MESH)
    for exists, peer in ends:

        @pl.when(exists)
        def _(peer=peer):
            pl.semaphore_signal(barrier, inc=1, device_id=peer, device_id_type=pl.DeviceIdType.MESH)

    waits = len(peers)
    if ends:
        me = lax.axis_index("space")
        waits = waits + jnp.minimum(me, 1) + jnp.minimum(lax.axis_size("space") - 1 - me, 1)
    pl.semaphore_wait(barrier, waits)


class Faces:
    def __init__(self, ends, head, tail, low, high, send, recv):
        (self.below, down), (self.above, up) = ends
        self.low, self.high = low, high
        self.down = pltpu.make_async_remote_copy(
            src_ref=head, dst_ref=high, send_sem=send.at[0], recv_sem=recv.at[0],
            device_id=down, device_id_type=pl.DeviceIdType.MESH,
        )
        self.up = pltpu.make_async_remote_copy(
            src_ref=tail, dst_ref=low, send_sem=send.at[1], recv_sem=recv.at[1],
            device_id=up, device_id_type=pl.DeviceIdType.MESH,
        )

    def start(self):
        pl.when(self.below)(self.down.start)
        pl.when(self.above)(self.up.start)

    def finish(self):
        @pl.when(self.below)
        def _():
            self.down.wait_send()
            self.up.wait_recv()

        @pl.when(jnp.logical_not(self.below))
        def _():
            self.low[...] = jnp.zeros(self.low.shape, self.low.dtype)

        @pl.when(self.above)
        def _():
            self.up.wait_send()
            self.down.wait_recv()

        @pl.when(jnp.logical_not(self.above))
        def _():
            self.high[...] = jnp.zeros(self.high.shape, self.high.dtype)


class Total:
    def __init__(self, order, start, size, held, landing, full, send, recv):
        self.held, self.landing, self.full, self.send, self.recv = held, landing, full, send, recv
        base = start
        self.plan = []
        for axis, bit in order:
            me = lax.axis_index(axis)
            half = size // 2
            mine = lax.rem(me // (1 << bit), 2)
            peer = {axis: me + (1 - 2 * mine) * (1 << bit)}
            keep = start + mine * half
            self.plan.append((peer, keep, start + (1 - mine) * half, half, base))
            start, size, base = keep, half, base + half
        self.copy, self.turn = None, -1

    def rows(self, start, size):
        return pl.ds(pl.multiple_of(start, 16), size)

    def run(self, turns):
        for _ in range(turns):
            if self.turn == 2 * len(self.plan):
                return
            if self.turn >= 0:
                self.end(self.turn)
            self.turn += 1
            if self.turn == 2 * len(self.plan):
                return
            self.begin(self.turn)

    def begin(self, turn):
        count = len(self.plan)
        if turn < count:
            peer, _, away, half, base = self.plan[turn]
            src = self.held.at[self.rows(away, half)]
            dst = self.landing.at[pl.ds(base, half)]
        else:
            peer, keep, _, half, _ = self.plan[2 * count - 1 - turn]
            if turn == count:
                self.full[self.rows(keep, half)] = self.held[self.rows(keep, half)]
            src = dst = self.full.at[self.rows(keep, half)]
        self.copy = pltpu.make_async_remote_copy(
            src_ref=src, dst_ref=dst, send_sem=self.send.at[turn], recv_sem=self.recv.at[turn],
            device_id=peer, device_id_type=pl.DeviceIdType.MESH,
        )
        self.copy.start()

    def end(self, turn):
        self.copy.wait()
        if turn < len(self.plan):
            _, keep, _, half, base = self.plan[turn]
            span = self.rows(keep, half)
            self.held[span] = (
                self.held[span].astype(F32) + self.landing[pl.ds(base, half)].astype(F32)
            ).astype(BF16)


def sum_orders(count, slabs):
    samples = [("sample", bit) for bit in range(count.bit_length() - 1)]
    spaces = [("space", bit) for bit in range(slabs.bit_length() - 1)]
    return samples[:2] + spaces + samples[2:], samples[:1] + spaces + samples[1:]


def mixed_body(
    count, slabs, width, partner_ref, share_ref, x_ref, kernel_ref,
    mate_ref, own_low, own_high, mate_low, mate_high, mixed_ref, low_ref, high_ref, slope_own_ref, slope_mate_ref,
    got_a, got_b, stage, hidden, store, wide_ref, send_one, recv_one, send_two, recv_two, send_face, recv_face,
):
    depth, cells, chans = x_ref.shape
    me = lax.axis_index("sample")
    peers = [lax.rem(me + step, count) for step in range(1, count)]
    ends = neighbours(slabs)
    greet([{"sample": peer} for peer in peers], ends)
    got = (got_a, got_b)
    piece = depth * cells // count
    per_layer = cells // piece
    rows = piece // 2

    def span(index, part):
        return index // per_layer, pl.ds(pl.multiple_of(lax.rem(index, per_layer) * piece + part * rows, 16), rows)

    def push(src, dst, send, recv, peer):
        return pltpu.make_async_remote_copy(
            src_ref=src, dst_ref=dst, send_sem=send, recv_sem=recv,
            device_id={"sample": peer}, device_id_type=pl.DeviceIdType.MESH,
        )

    def faces(block, edge, low, high, kind):
        return Faces(
            ends, block.at[pl.ds(0, edge)], block.at[pl.ds(depth - edge, edge)], low, high,
            send_face.at[kind], recv_face.at[kind],
        )

    first, second = [], []
    for part in range(2):
        first.append([
            push(x_ref.at[span(peer, part)], got[part].at[me], send_one.at[part, place], recv_one.at[part, place], peer)
            for place, peer in enumerate(peers)
        ])
        for copy in first[part]:
            copy.start()
        if part == 0:
            own = faces(x_ref, 1, own_low, own_high, 0)
            own.start()
    share = share_ref[me]
    fill_pairs(kernel_ref, wide_ref)
    frame_all(store, None, x_ref, None, 1, width, range(1, depth + 1))
    own.finish()
    frame_all(store, own_low, x_ref, own_high, 1, width, (0, depth + 1))
    for p, value in conv_pairs(store, wide_ref, depth, 1, width, cells):
        squash = jax.nn.sigmoid(value)
        hidden[p] = (value * squash).astype(BF16)
        slope_own_ref[p] = share * (squash * (1.0 + value * (1.0 - squash)))
    for part in range(2):
        got[part][me] = x_ref[span(me, part)]
        for copy in first[part]:
            copy.wait_recv()
        second.append([])
        for place, peer in enumerate(peers):
            stage[part, place] = got[part][partner_ref[peer]]
            copy = push(
                stage.at[part, place], mate_ref.at[span(me, part)],
                send_two.at[part, place], recv_two.at[part, place], peer,
            )
            copy.start()
            second[part].append(copy)
        mate_ref[span(me, part)] = got[part][partner_ref[me]]
    for copies in second:
        for copy in copies:
            copy.wait_recv()
    mates = faces(mate_ref, 1, mate_low, mate_high, 1)
    mates.start()
    frame_all(store, None, mate_ref, None, 1, width, range(1, depth + 1))
    mates.finish()
    frame_all(store, mate_low, mate_ref, mate_high, 1, width, (0, depth + 1))
    for p, value in conv_pairs(store, wide_ref, depth, 1, width, cells):
        squash = jax.nn.sigmoid(value)
        other = (value * squash).astype(BF16).astype(F32)
        mixed_ref[p] = (share * hidden[p].astype(F32) + (1.0 - share) * other).astype(BF16)
        slope_mate_ref[p] = (1.0 - share) * (squash * (1.0 + value * (1.0 - squash)))
    mixes = faces(mixed_ref, 2, low_ref, high_ref, 2)
    mixes.start()
    for copies in first + second:
        for copy in copies:
            copy.wait_send()
    mixes.finish()


def mixed_call(x, kernel, partner, coefficient, count, slabs, width):
    depth, cells, chans = x.shape
    rows = depth * cells // count // 2
    dma = pltpu.SemaphoreType.DMA
    vmem = pl.BlockSpec(memory_space=pltpu.VMEM)
    smem = pl.BlockSpec(memory_space=pltpu.SMEM)

    def layers(n, dtype=BF16):
        return jax.ShapeDtypeStruct((n, cells, chans), dtype)

    return pl.pallas_call(
        functools.partial(mixed_body, count, slabs, width),
        out_shape=[layers(depth)] + [layers(1)] * 4 + [layers(depth), layers(2), layers(2)] + [layers(depth, F32)] * 2,
        in_specs=[smem, smem, vmem, vmem],
        out_specs=[vmem] * 10,
        scratch_shapes=[
            pltpu.VMEM((count, rows, chans), BF16),
            pltpu.VMEM((count, rows, chans), BF16),
            pltpu.VMEM((2, count - 1, rows, chans), BF16),
            pltpu.VMEM((depth, cells, chans), BF16),
            pltpu.VMEM((depth + 2, cells + 2 * width, 3 * chans), BF16),
            pltpu.VMEM((4, 9 * chans, 2 * chans), BF16),
            dma((2, count - 1)), dma((2, count - 1)), dma((2, count - 1)), dma((2, count - 1)),
            dma((3, 2)), dma((3, 2)),
        ],
        compiler_params=pltpu.CompilerParams(
            collective_id=0, has_side_effects=True, vmem_limit_bytes=VMEM_LIMIT
        ),
    )(partner, coefficient, x, kernel)


def grads_body(
    count, slabs, width, low_ref, mixed_ref, high_ref, grad_ref, kernel_ref, slope_own_ref, slope_mate_ref,
    own_low, own_ref, own_high, mate_low, mate_ref, mate_high, out_one, out_two,
    grad_low, grad_high, store_two, store_one, wide_ref, term_own, term_mate, total,
    held_one, held_two, land_one, land_two, full_one, full_two, send, recv, send_face, recv_face,
):
    depth, cells, chans = grad_ref.shape
    orders = sum_orders(count, slabs)
    peers = []
    for axis, bit in orders[0]:
        me = lax.axis_index(axis)
        peers.append({axis: me + (1 - 2 * lax.rem(me // (1 << bit), 2)) * (1 << bit)})
    ends = neighbours(slabs)
    greet(peers, ends)
    size = held_one.shape[0]
    used = 27 * chans
    unit = 16 * count * slabs
    cut = (size // unit + 1) // 2 * unit

    def lanes(kind, held, land, full):
        made = []
        for lane, (start, end) in enumerate(((0, cut), (cut, size))):
            if end > start:
                made.append(
                    Total(orders[lane], start, end - start, held, land, full, send.at[kind, lane], recv.at[kind, lane])
                )
        return made

    def advance(made, turns=1):
        for _ in range(turns):
            for lane in made:
                lane.run(1)

    def hand_over(held):
        for tap in range(3):
            held[pl.ds(tap * 9 * chans, 9 * chans)] = total[tap].astype(BF16)
        if size > used:
            held[pl.ds(used, size - used)] = jnp.zeros((size - used, chans), BF16)

    faces = Faces(
        ends, grad_ref.at[pl.ds(0, 2)], grad_ref.at[pl.ds(depth - 2, 2)], grad_low, grad_high, send_face, recv_face
    )
    faces.start()

    def grad_at(ref, p):
        return jnp.zeros((cells, chans), BF16) if p is None else ref[p]

    frame_all(store_two, low_ref, mixed_ref, high_ref, 2, width)
    total[...] = jnp.zeros_like(total)
    for tap, part in grad_blocks(store_two, functools.partial(grad_at, grad_ref), depth, 2, width, cells):
        total[tap] += part
    hand_over(held_two)
    seconds = lanes(1, held_two, land_two, full_two)
    advance(seconds)
    fill_back(kernel_ref, wide_ref)
    frame_all(store_two, None, grad_ref, None, 2, width, range(2, depth + 2))
    faces.finish()
    frame_all(store_two, grad_low, grad_ref, grad_high, 2, width, (0, 1, depth + 2, depth + 3))
    advance(seconds)
    for p, value in conv_pairs(store_two, wide_ref, depth, 2, width, cells, back=True):
        value = value.astype(BF16).astype(F32)
        term_own[p] = (value * slope_own_ref[p]).astype(BF16)
        term_mate[p] = (value * slope_mate_ref[p]).astype(BF16)
    advance(seconds)
    total[...] = jnp.zeros_like(total)
    for slab, term in (((own_low, own_ref, own_high), term_own), ((mate_low, mate_ref, mate_high), term_mate)):
        frame_all(store_one, *slab, 1, width)
        advance(seconds)
        for tap, part in grad_blocks(store_one, functools.partial(grad_at, term), depth, 1, width, cells):
            total[tap] += part
            if tap == 2:
                advance(seconds)
    hand_over(held_one)
    firsts = lanes(0, held_one, land_one, full_one)
    for _ in range(2 * len(orders[0]) + 1):
        advance(firsts)
        advance(seconds)
    out_one[...] = full_one[pl.ds(0, used)]
    out_two[...] = full_two[pl.ds(0, used)]


def grads_call(args, count, slabs, width):
    depth, cells, chans = args[3].shape
    used = 27 * chans
    size = used + -used % (16 * count * slabs)
    turns = 2 * len(sum_orders(count, slabs)[0])
    vmem = pl.BlockSpec(memory_space=pltpu.VMEM)
    dma = pltpu.SemaphoreType.DMA
    buffer = pltpu.VMEM((size, chans), BF16)
    return pl.pallas_call(
        functools.partial(grads_body, count, slabs, width),
        out_shape=[jax.ShapeDtypeStruct((used, chans), BF16)] * 2,
        in_specs=[vmem] * len(args),
        out_specs=[vmem] * 2,
        scratch_shapes=[
            pltpu.VMEM((2, cells, chans), BF16),
            pltpu.VMEM((2, cells, chans), BF16),
            pltpu.VMEM((depth + 4, cells + 4 * width, 3 * chans), BF16),
            pltpu.VMEM((depth + 2, cells + 2 * width, 3 * chans), BF16),
            pltpu.VMEM((4, 2 * chans, 9 * chans), BF16),
            pltpu.VMEM((depth, cells, chans), BF16),
            pltpu.VMEM((depth, cells, chans), BF16),
            pltpu.VMEM((3, 9 * chans, chans), F32),
        ]
        + [buffer] * 6
        + [dma((2, 2, turns)), dma((2, 2, turns)), dma((2,)), dma((2,))],
        compiler_params=pltpu.CompilerParams(
            collective_id=1, has_side_effects=True, vmem_limit_bytes=VMEM_LIMIT
        ),
    )(*args)


def shards(volume, first_kernel, second_kernel, partner, coefficient, out_grad):
    _, depth, height, width, chans = volume.shape
    cells = height * width
    count, slabs = lax.axis_size("sample"), lax.axis_size("space")
    x = volume.reshape(depth, cells, chans)
    cot = out_grad.reshape(depth, cells, chans)
    flat_one = first_kernel.reshape(3, 9 * chans, chans)
    flat_two = second_kernel.reshape(3, 9 * chans, chans)
    mate, own_low, own_high, mate_low, mate_high, mixed, low, high, slope_own, slope_mate = mixed_call(
        x, flat_one, partner, coefficient, count, slabs, width
    )
    half = jax.ShapeDtypeStruct((depth, cells, chans), BF16)
    result, grad_two = call(
        second_body,
        width,
        (low, mixed, high, flat_two, cot),
        (half, half),
        [
            pltpu.VMEM((depth + 4, cells + 4 * width, 3 * chans), BF16),
            pltpu.VMEM((4, 9 * chans, 2 * chans), BF16),
        ],
        2 * depth * cells * 27 * chans * chans,
    )
    first_sum, second_sum = grads_call(
        (low, mixed, high, grad_two, flat_two, slope_own, slope_mate, own_low, x, own_high, mate_low, mate, mate_high),
        count,
        slabs,
        width,
    )
    shape = first_kernel.shape
    return (
        result.reshape(volume.shape),
        first_sum.astype(F32).reshape(shape),
        second_sum.astype(F32).reshape(shape),
    )


def solution(mesh):
    in_specs = (
        P("sample", "space", None, None, None),
        P(),
        P(),
        P(),
        P(),
        P("sample", "space", None, None, None),
    )
    out_specs = (P("sample", "space", None, None, None), P(), P())
    return jax.shard_map(shards, mesh=mesh, in_specs=in_specs, out_specs=out_specs, check_vma=False)
```

time: 151 us -> 129 us (0.85)
  local copies, waits for them, and re-layouts: 11.9 us -> 0.01 us
  starting transfers between devices: 6.64 us -> 0 us
  waiting for transfers between devices: 3.77 us -> 0 us
    pallas_call x2, Pallas kernels: 84.1 us -> 118 us  [the longest x1 72.9 us: grads_call(): pl.pallas_call(functools.partial(grads_body, count, slabs, width), out_sh...]
    pallas_call x5 -> x1, Pallas kernels: 38.5 us -> 5.57 us  [call(): pl.pallas_call(functools.partial(body, width), out_shape=outs, in_specs=[...]
    ppermute x4 -> x0, starting transfers between devices: 6.64 us -> none  [the longest x2 3.88 us: edges(): lax.ppermute(block[-width:], 'space', [(i, i + 1) for i in range(count -...]
    pad x2 -> x0, local copies, waits for them, and re-layouts: 4.3 us -> none  [shards(): jnp.pad(a.reshape(rows, chans), ((0, spare), (0, 0)))]
    ppermute x4 -> x0, waiting for transfers between devices: 3.77 us -> none  [the longest x2 3.77 us: edges(): lax.ppermute(block[:width], 'space', [(i + 1, i) for i in range(count - 1)])]
    slice x4 -> x0, local copies, waits for them, and re-layouts: 3.25 us -> none  [the longest x2 1.97 us: edges(): block[:width]]
    transpose x2 -> x0, local copies, waits for them, and re-layouts: 1.77 us -> none  [shards(): jnp.transpose(jnp.flip(second_kernel, (0, 1, 2)), (0, 1, 2, 4, 3))]
  transfers between devices with their start and end apart: 4 -> 0, of which waited for: 1 -> 0; matrix products, arithmetic and copies ran while one was open for 3% -> 0% of each run, Pallas kernels for 3% -> 0%
where the time goes in v3:
time: 129 us; the launch traced here: 128 us
  Pallas kernels  124 us (96%)
  other arithmetic  4.07 us (3%)
    pallas_call x1, Pallas kernels, grads_call(): pl.pallas_call(functools.partial(grads_body, count, slabs, width), out_sh...  72.9 us
    pallas_call x1, Pallas kernels, mixed_call(): pl.pallas_call(functools.partial(mixed_body, count, slabs, width), out_sh...  45.2 us
    pallas_call x1, Pallas kernels, call(): pl.pallas_call(functools.partial(body, width), out_shape=outs, in_specs=[...  5.57 us
    reshape x1, other arithmetic, shards(): first_sum.astype(F32).reshape(shape)  2.66 us

profile of v3, /device:TPU:0, one launch (start us, length us, event | category | flops | bytes accessed | tf_op | source)
XLA Modules:
  0.0 128.4 jit_solution(14817566109527509036)
XLA Ops:
  0.6 45.2 %shard_map.85 = (bf16[8,256,128]{2,1,0:T(8,128)(2,1)}, bf16[1,256,128]{2,1,0:T(8,128)(2,1)}, bf16[1,256,128]{2,1,0:T(8,128)(2,1)}, bf16[1,256,128]{2,1,0:T(8,128...) custom-call(s32[16]{0:T(128)} %partner_ref.1, ...), custom_call_target="tpu_custom_call" | custom-call | tf_op jit(solution)/shard_map/pallas_call | solution.py:374
  45.8 5.6 %shard_map.86 = (bf16[8,256,128]{2,1,0:T(8,128)(2,1)}, bf16[8,256,128]{2,1,0:T(8,128)(2,1)}) custom-call(bf16[2,256,128]{2,1,0:T(8,128)(2,1)} %get-tuple-element.17.low_ref, bf16[8,256,128]{2,1,0:T(8,128)(2,1)} %get-tuple-element.18.mixed_ref, bf16[2,256,128]{2,1,0:T(8,128)(2,1)} %get-tuple-element.19.high_ref, bf16[3,1152,128]{2,1,0:T(8,128)(2,1)} %bitcast.14, ...), custom_call_target="tpu_custom_call" | custom-call | flops 1811939328 | bytes 2195456 | tf_op jit(solution)/shard_map/pallas_call | solution.py:147
  51.4 72.9 %shard_map.87 = (bf16[3456,128]{1,0:T(8,128)(2,1)}, bf16[3456,128]{1,0:T(8,128)(2,1)}) custom-call(bf16[2,256,128]{2,1,0:T(8,128)(2,1)} %get-tuple-element.17.low_ref, bf16[8,256,128]{2,1,0:T(8,128)(2,1)} %get-tuple-element.18.mixed_ref, bf16[2,256,128]{2,1,0:T(8,128)(2,1)} %get-tuple-element.19.high_ref, bf16[8,256,128]{2,1,0:T(8,128)(2,1)} %get-tuple-element.21.grad_ref, ...), custom_call_target="tpu_custom_call" | custom-call | tf_op jit(solution)/shard_map/pallas_call | solution.py:484
  124.3 0.0 copy-start
  124.3 2.7 %convert.2 = f32[3,3,3,128,128]{4,3,2,1,0:T(8,128)} convert(bf16[3,3,3,128,128]{4,3,2,1,0:T(8,128)(2,1)} %bitcast.13) | non-fusion elementwise | flops 442368 | bytes 2654208 | tf_op jit(solution)/shard_map/reshape | solution.py:539
  127.0 0.0 copy-done
  127.0 1.4 %convert.3 = f32[3,3,3,128,128]{4,3,2,1,0:T(8,128)} convert(bf16[3,3,3,128,128]{4,3,2,1,0:T(8,128)(2,1)S(1)} %bitcast.12) | non-fusion elementwise | flops 442368 | bytes 2654208 | tf_op jit(solution)/shard_map/reshape | solution.py:540
Async XLA Ops:
  124.3 2.7 %copy-start = (bf16[3456,128]{1,0:T(8,128)(2,1)S(1)}, bf16[3456,128]{1,0:T(8,128)(2,1)}, u32[]{:S(2)}) copy-start(bf16[3456,128]{1,0:T(8,128)(2,1)} %get-tuple-element.30) | copy-start | bytes 2654212

commit v4 on v3

v4 whole, which is shorter than its diff:
```python
import functools

import jax
import jax.numpy as jnp
from jax import lax
from jax.experimental import pallas as pl
from jax.experimental.pallas import tpu as pltpu
from jax.sharding import PartitionSpec as P

F32 = jnp.float32
BF16 = jnp.bfloat16
VMEM_LIMIT = 56 * 1024 * 1024


def slope(value):
    squash = jax.nn.sigmoid(value)
    return squash * (1.0 + value * (1.0 - squash))


def groups(depth, spread):
    return [p for p in range(depth) if (p // spread) % 2 == 0]


def frame(store, layer, plane, spread, width):
    cells, chans = plane.shape
    edge = spread * width
    wide = plane.astype(F32)
    column = lax.broadcasted_iota(jnp.int32, plane.shape, 0) % width
    left = jnp.where(column >= spread, pltpu.roll(wide, spread, 0), 0.0).astype(BF16)
    right = jnp.where(column < width - spread, pltpu.roll(wide, cells - spread, 0), 0.0).astype(BF16)
    store[layer, pl.ds(0, edge), :] = jnp.zeros((edge, 3 * chans), BF16)
    store[layer, pl.ds(edge + cells, edge), :] = jnp.zeros((edge, 3 * chans), BF16)
    for place, value in enumerate((left, plane, right)):
        store[layer, pl.ds(edge, cells), pl.ds(place * chans, chans)] = value


def taps(store, layer, spread, width, cells):
    return jnp.concatenate(
        [store[layer, pl.ds(row * spread * width, cells), :] for row in range(3)], axis=1
    )


def fill_pairs(kernel_ref, wide_ref):
    chans = kernel_ref.shape[2]
    for step in range(4):
        for out in range(2):
            depth_tap = step - out
            block = (
                kernel_ref[depth_tap]
                if 0 <= depth_tap < 3
                else jnp.zeros(kernel_ref.shape[1:], BF16)
            )
            wide_ref[step, :, pl.ds(out * chans, chans)] = block


def fill_back(kernel_ref, wide_ref):
    chans = kernel_ref.shape[2]
    for step in range(4):
        for out in range(2):
            depth_tap = step - out
            for place in range(9):
                block = (
                    kernel_ref[2 - depth_tap, pl.ds((8 - place) * chans, chans)]
                    if 0 <= depth_tap < 3
                    else jnp.zeros((chans, chans), BF16)
                )
                wide_ref[step, pl.ds(out * chans, chans), pl.ds(place * chans, chans)] = block


def conv_pairs(store, wide_ref, first, spread, width, cells, back=False):
    side = 1 if back else 0
    total = None
    for half in range(2):
        rows = []
        for p in first:
            rows.append(
                jnp.concatenate(
                    [
                        taps(store, p + spread * (2 * half + k), spread, width, cells)
                        for k in range(2)
                    ],
                    axis=1,
                )
            )
        lhs = jnp.concatenate(rows, axis=0)
        rhs = jnp.concatenate([wide_ref[2 * half], wide_ref[2 * half + 1]], axis=side)
        part = lax.dot_general(lhs, rhs, (((1,), (side,)), ((), ())), preferred_element_type=F32)
        total = part if total is None else total + part
    chans = total.shape[1] // 2
    for place, p in enumerate(first):
        for out in range(2):
            yield p + out * spread, total[
                place * cells : (place + 1) * cells, out * chans : (out + 1) * chans
            ]


def grad_blocks(store, grad_at, depth, spread, width, cells):
    ranges = ((0, 2 * spread, (0, 1)), (2 * spread, depth, (0, 1, 2)), (depth, depth + 2 * spread, (1, 2)))
    for low, high, depth_taps in ranges:
        lhs = jnp.concatenate(
            [taps(store, e, spread, width, cells) for e in range(low, high)], axis=0
        )
        columns = []
        for tap in depth_taps:
            layers = []
            for e in range(low, high):
                p = e - spread * tap
                layers.append(grad_at(p if 0 <= p < depth else None))
            columns.append(jnp.concatenate(layers, axis=0))
        rhs = jnp.concatenate(columns, axis=1)
        part = lax.dot_general(lhs, rhs, (((0,), (0,)), ((), ())), preferred_element_type=F32)
        chans = columns[0].shape[1]
        for place, tap in enumerate(depth_taps):
            yield tap, part[:, place * chans : (place + 1) * chans]


def frame_all(store, low_ref, x_ref, high_ref, spread, width, layers=None):
    depth = x_ref.shape[0]
    for layer in range(depth + 2 * spread) if layers is None else layers:
        if layer < spread:
            plane = low_ref[layer]
        elif layer < depth + spread:
            plane = x_ref[layer - spread]
        else:
            plane = high_ref[layer - depth - spread]
        frame(store, layer, plane, spread, width)


def neighbours(count):
    me = lax.axis_index("space")
    return (me > 0, {"space": me - 1}), (me < count - 1, {"space": me + 1})


def greet(peers, ends):
    barrier = pltpu.get_barrier_semaphore()
    for peer in peers:
        pl.semaphore_signal(barrier, inc=1, device_id=peer, device_id_type=pl.DeviceIdType.MESH)
    for exists, peer in ends:

        @pl.when(exists)
        def _(peer=peer):
            pl.semaphore_signal(barrier, inc=1, device_id=peer, device_id_type=pl.DeviceIdType.MESH)

    waits = len(peers)
    if ends:
        me = lax.axis_index("space")
        waits = waits + jnp.minimum(me, 1) + jnp.minimum(lax.axis_size("space") - 1 - me, 1)
    pl.semaphore_wait(barrier, waits)


class Faces:
    def __init__(self, ends, head, tail, low, high, send, recv):
        (self.below, down), (self.above, up) = ends
        self.low, self.high = low, high
        self.down = pltpu.make_async_remote_copy(
            src_ref=head, dst_ref=high, send_sem=send.at[0], recv_sem=recv.at[0],
            device_id=down, device_id_type=pl.DeviceIdType.MESH,
        )
        self.up = pltpu.make_async_remote_copy(
            src_ref=tail, dst_ref=low, send_sem=send.at[1], recv_sem=recv.at[1],
            device_id=up, device_id_type=pl.DeviceIdType.MESH,
        )

    def start(self):
        pl.when(self.below)(self.down.start)
        pl.when(self.above)(self.up.start)

    def finish(self):
        @pl.when(self.below)
        def _():
            self.down.wait_send()
            self.up.wait_recv()

        @pl.when(jnp.logical_not(self.below))
        def _():
            self.low[...] = jnp.zeros(self.low.shape, self.low.dtype)

        @pl.when(self.above)
        def _():
            self.up.wait_send()
            self.down.wait_recv()

        @pl.when(jnp.logical_not(self.above))
        def _():
            self.high[...] = jnp.zeros(self.high.shape, self.high.dtype)


class Total:
    def __init__(self, order, start, size, held, landing, full, send, recv):
        self.held, self.landing, self.full, self.send, self.recv = held, landing, full, send, recv
        base = start
        self.plan = []
        for axis, low, members in order:
            me = lax.axis_index(axis)
            place = lax.rem(me // low, members)
            part = size // members
            others = []
            for step in range(1, members):
                other = lax.rem(place + step, members)
                others.append(({axis: me + (other - place) * low}, start + other * part, base))
                base += part
            start, size = start + place * part, part
            self.plan.append((others, start, part))
        self.copies, self.turn = [], -1

    def rows(self, start, size):
        return pl.ds(pl.multiple_of(start, 16), size)

    def advance(self):
        if self.turn == 2 * len(self.plan):
            return
        if self.turn >= 0:
            self.end(self.turn)
        self.turn += 1
        if self.turn < 2 * len(self.plan):
            self.begin(self.turn)

    def begin(self, turn):
        count = len(self.plan)
        scatter = turn < count
        others, keep, part = self.plan[turn if scatter else 2 * count - 1 - turn]
        if turn == count:
            self.full[self.rows(keep, part)] = self.held[self.rows(keep, part)]
        self.copies = []
        for place, (peer, away, base) in enumerate(others):
            if scatter:
                src, dst = self.held.at[self.rows(away, part)], self.landing.at[pl.ds(base, part)]
            else:
                src = dst = self.full.at[self.rows(keep, part)]
            copy = pltpu.make_async_remote_copy(
                src_ref=src, dst_ref=dst, send_sem=self.send.at[turn, place], recv_sem=self.recv.at[turn, place],
                device_id=peer, device_id_type=pl.DeviceIdType.MESH,
            )
            copy.start()
            self.copies.append(copy)

    def end(self, turn):
        for copy in self.copies:
            copy.wait()
        if turn < len(self.plan):
            others, keep, part = self.plan[turn]
            span = self.rows(keep, part)
            value = self.held[span].astype(F32)
            for _, _, base in others:
                value = value + self.landing[pl.ds(base, part)].astype(F32)
            self.held[span] = value.astype(BF16)


def stages(axis, first, last):
    made = []
    while first < last:
        bits = min(2, last - first)
        made.append((axis, 1 << first, 1 << bits))
        first += bits
    return made


def sum_orders(count, slabs):
    bits = count.bit_length() - 1
    core = stages("sample", 0, min(1, bits))
    near = stages("sample", min(1, bits), min(2, bits))
    far = stages("sample", min(2, bits), bits)
    spaces = stages("space", 0, slabs.bit_length() - 1)
    return core + near + spaces + far, core + spaces + near + far


def whole_body(
    count, slabs, width, partner_ref, share_ref, x_ref, kernel_one_ref, kernel_two_ref, cot_ref,
    result_ref, out_one, out_two,
    got_a, got_b, stage, hidden, mate_ref, faces_one, faces_two, mixed_ref, grad_ref, slope_own_ref, slope_mate_ref,
    store_own, store_mate, store_mix, store_grad, wide_one, wide_two, wide_back, term_own, term_mate, total,
    held_one, held_two, land_one, land_two, full_one, full_two,
    send_one, recv_one, send_two, recv_two, send_face, recv_face, send, recv,
):
    depth, cells, chans = x_ref.shape
    me = lax.axis_index("sample")
    peers = [lax.rem(me + step, count) for step in range(1, count)]
    ends = neighbours(slabs)
    orders = sum_orders(count, slabs)
    far = []
    for axis, low, members in orders[0]:
        if axis == "space":
            at = lax.axis_index(axis)
            place = lax.rem(at // low, members)
            far += [{axis: at + (lax.rem(place + step, members) - place) * low} for step in range(1, members)]
    greet([{"sample": peer} for peer in peers] + far, ends)
    got = (got_a, got_b)
    piece = depth * cells // count
    per_layer = cells // piece
    rows = piece // 2

    def span(index, part):
        return index // per_layer, pl.ds(pl.multiple_of(lax.rem(index, per_layer) * piece + part * rows, 16), rows)

    def push(src, dst, send, recv, peer):
        return pltpu.make_async_remote_copy(
            src_ref=src, dst_ref=dst, send_sem=send, recv_sem=recv,
            device_id={"sample": peer}, device_id_type=pl.DeviceIdType.MESH,
        )

    def faces(block, edge, low, high, kind):
        return Faces(
            ends, block.at[pl.ds(0, edge)], block.at[pl.ds(depth - edge, edge)], low, high,
            send_face.at[kind], recv_face.at[kind],
        )

    own_low, own_high, mate_low, mate_high = [faces_one.at[pl.ds(k, 1)] for k in range(4)]
    mix_low, mix_high, grad_low, grad_high = [faces_two.at[pl.ds(2 * k, 2)] for k in range(4)]

    first, second = [], []
    for part in range(2):
        first.append([
            push(x_ref.at[span(peer, part)], got[part].at[me], send_one.at[part, place], recv_one.at[part, place], peer)
            for place, peer in enumerate(peers)
        ])
        for copy in first[part]:
            copy.start()
        if part == 0:
            own = faces(x_ref, 1, own_low, own_high, 0)
            own.start()
    share = share_ref[me]
    fill_pairs(kernel_one_ref, wide_one)
    frame_all(store_own, None, x_ref, None, 1, width, range(1, depth + 1))
    for part in range(2):
        got[part][me] = x_ref[span(me, part)]
        for copy in first[part]:
            copy.wait_recv()
        second.append([])
        for place, peer in enumerate(peers):
            stage[part, place] = got[part][partner_ref[peer]]
            copy = push(
                stage.at[part, place], mate_ref.at[span(me, part)],
                send_two.at[part, place], recv_two.at[part, place], peer,
            )
            copy.start()
            second[part].append(copy)
        mate_ref[span(me, part)] = got[part][partner_ref[me]]

    own.finish()
    frame_all(store_own, own_low, x_ref, own_high, 1, width, (0, depth + 1))
    for p, value in conv_pairs(store_own, wide_one, groups(depth, 1), 1, width, cells):
        squash = jax.nn.sigmoid(value)
        hidden[p] = (value * squash).astype(BF16)
        slope_own_ref[p] = share * (squash * (1.0 + value * (1.0 - squash)))
    fill_pairs(kernel_two_ref, wide_two)
    fill_back(kernel_two_ref, wide_back)
    for copies in second:
        for copy in copies:
            copy.wait_recv()
    mates = faces(mate_ref, 1, mate_low, mate_high, 1)
    mates.start()
    frame_all(store_mate, None, mate_ref, None, 1, width, range(1, depth + 1))
    mates.finish()
    frame_all(store_mate, mate_low, mate_ref, mate_high, 1, width, (0, depth + 1))

    def mix(pairs):
        for p, value in conv_pairs(store_mate, wide_one, pairs, 1, width, cells):
            squash = jax.nn.sigmoid(value)
            other = (value * squash).astype(BF16).astype(F32)
            mixed_ref[p] = (share * hidden[p].astype(F32) + (1.0 - share) * other).astype(BF16)
            slope_mate_ref[p] = (1.0 - share) * (squash * (1.0 + value * (1.0 - squash)))

    pairs = groups(depth, 1)
    mix([pairs[0], pairs[-1]])
    mixes = faces(mixed_ref, 2, mix_low, mix_high, 2)
    mixes.start()
    mix(pairs[1:-1])
    frame_all(store_mix, None, mixed_ref, None, 2, width, range(2, depth + 2))
    for copies in first + second:
        for copy in copies:
            copy.wait_send()
    mixes.finish()
    frame_all(store_mix, mix_low, mixed_ref, mix_high, 2, width, (0, 1, depth + 2, depth + 3))

    for p, value in conv_pairs(store_mix, wide_two, groups(depth, 2), 2, width, cells):
        squash = jax.nn.sigmoid(value)
        result_ref[p] = (value * squash).astype(BF16)
        grad_ref[p] = (cot_ref[p].astype(F32) * (squash * (1.0 + value * (1.0 - squash)))).astype(BF16)
    backs = faces(grad_ref, 2, grad_low, grad_high, 3)
    backs.start()

    size = held_one.shape[0]
    used = 27 * chans
    unit = 16 * count * slabs
    cut = (size // unit + 1) // 2 * unit

    def lanes(kind, held, land, full):
        made = []
        for lane, (start, end) in enumerate(((0, cut), (cut, size))):
            if end > start:
                made.append(
                    Total(orders[lane], start, end - start, held, land, full, send.at[kind, lane], recv.at[kind, lane])
                )
        return made

    def advance(made):
        for lane in made:
            lane.advance()

    def hand_over(held):
        for tap in range(3):
            held[pl.ds(tap * 9 * chans, 9 * chans)] = total[tap].astype(BF16)
        if size > used:
            held[pl.ds(used, size - used)] = jnp.zeros((size - used, chans), BF16)

    def grad_at(ref, p):
        return jnp.zeros((cells, chans), BF16) if p is None else ref[p]

    total[...] = jnp.zeros_like(total)
    for tap, part in grad_blocks(store_mix, functools.partial(grad_at, grad_ref), depth, 2, width, cells):
        total[tap] += part
    hand_over(held_two)
    seconds = lanes(1, held_two, land_two, full_two)
    advance(seconds)
    frame_all(store_grad, None, grad_ref, None, 2, width, range(2, depth + 2))
    backs.finish()
    frame_all(store_grad, grad_low, grad_ref, grad_high, 2, width, (0, 1, depth + 2, depth + 3))
    for p, value in conv_pairs(store_grad, wide_back, groups(depth, 2), 2, width, cells, back=True):
        value = value.astype(BF16).astype(F32)
        term_own[p] = (value * slope_own_ref[p]).astype(BF16)
        term_mate[p] = (value * slope_mate_ref[p]).astype(BF16)
    advance(seconds)
    total[...] = jnp.zeros_like(total)
    for store, term in ((store_own, term_own), (store_mate, term_mate)):
        for tap, part in grad_blocks(store, functools.partial(grad_at, term), depth, 1, width, cells):
            total[tap] += part
        advance(seconds)
    hand_over(held_one)
    firsts = lanes(0, held_one, land_one, full_one)
    for _ in range(2 * len(orders[0]) + 1):
        advance(firsts)
        advance(seconds)
    out_one[...] = full_one[pl.ds(0, used)]
    out_two[...] = full_two[pl.ds(0, used)]


def whole_call(args, count, slabs, width):
    depth, cells, chans = args[2].shape
    rows = depth * cells // count // 2
    used = 27 * chans
    size = used + -used % (16 * count * slabs)
    turns = 2 * len(sum_orders(count, slabs)[0])
    vmem = pl.BlockSpec(memory_space=pltpu.VMEM)
    smem = pl.BlockSpec(memory_space=pltpu.SMEM)
    dma = pltpu.SemaphoreType.DMA
    slab = pltpu.VMEM((depth, cells, chans), BF16)
    wide_slab = pltpu.VMEM((depth, cells, chans), F32)
    sums = jax.ShapeDtypeStruct((used, chans), BF16)
    return pl.pallas_call(
        functools.partial(whole_body, count, slabs, width),
        out_shape=[jax.ShapeDtypeStruct((depth, cells, chans), BF16), sums, sums],
        in_specs=[smem, smem] + [vmem] * 4,
        out_specs=[vmem] * 3,
        scratch_shapes=[
            pltpu.VMEM((count, rows, chans), BF16),
            pltpu.VMEM((count, rows, chans), BF16),
            pltpu.VMEM((2, count - 1, rows, chans), BF16),
            slab,
            slab,
            pltpu.VMEM((4, cells, chans), BF16),
            pltpu.VMEM((8, cells, chans), BF16),
            slab,
            slab,
            wide_slab,
            wide_slab,
            pltpu.VMEM((depth + 2, cells + 2 * width, 3 * chans), BF16),
            pltpu.VMEM((depth + 2, cells + 2 * width, 3 * chans), BF16),
            pltpu.VMEM((depth + 4, cells + 4 * width, 3 * chans), BF16),
            pltpu.VMEM((depth + 4, cells + 4 * width, 3 * chans), BF16),
            pltpu.VMEM((4, 9 * chans, 2 * chans), BF16),
            pltpu.VMEM((4, 9 * chans, 2 * chans), BF16),
            pltpu.VMEM((4, 2 * chans, 9 * chans), BF16),
            slab,
            slab,
            pltpu.VMEM((3, 9 * chans, chans), F32),
        ]
        + [pltpu.VMEM((size, chans), BF16)] * 6
        + [dma((2, count - 1))] * 4
        + [dma((4, 2))] * 2
        + [dma((2, 2, turns, 3))] * 2,
        compiler_params=pltpu.CompilerParams(
            collective_id=0, has_side_effects=True, vmem_limit_bytes=VMEM_LIMIT
        ),
    )(*args)


def shards(volume, first_kernel, second_kernel, partner, coefficient, out_grad):
    _, depth, height, width, chans = volume.shape
    cells = height * width
    count, slabs = lax.axis_size("sample"), lax.axis_size("space")
    result, first_sum, second_sum = whole_call(
        (
            partner,
            coefficient,
            volume.reshape(depth, cells, chans),
            first_kernel.reshape(3, 9 * chans, chans),
            second_kernel.reshape(3, 9 * chans, chans),
            out_grad.reshape(depth, cells, chans),
        ),
        count,
        slabs,
        width,
    )
    shape = first_kernel.shape
    return (
        result.reshape(volume.shape),
        first_sum.astype(F32).reshape(shape),
        second_sum.astype(F32).reshape(shape),
    )


def solution(mesh):
    in_specs = (
        P("sample", "space", None, None, None),
        P(),
        P(),
        P(),
        P(),
        P("sample", "space", None, None, None),
    )
    out_specs = (P("sample", "space", None, None, None), P(), P())
    return jax.shard_map(shards, mesh=mesh, in_specs=in_specs, out_specs=out_specs, check_vma=False)
```

time: 129 us -> 106 us (0.82)
  Pallas kernels: 124 us -> 101 us
    pallas_call x3 -> x1, Pallas kernels: 124 us -> 101 us  [whole_call(): pl.pallas_call(functools.partial(whole_body, count, slabs, width), out_sh...]
where the time goes in v4:
time: 106 us
  Pallas kernels  101 us (95%)
  other arithmetic  4.07 us (4%)
    pallas_call x1, Pallas kernels, whole_call(): pl.pallas_call(functools.partial(whole_body, count, slabs, width), out_sh...  101 us
    reshape x1, other arithmetic, shards(): first_sum.astype(F32).reshape(shape)  2.66 us

profile of v4, /device:TPU:0, one launch (start us, length us, event | category | flops | bytes accessed | tf_op | source)
XLA Modules:
  0.0 106.1 jit_solution(15410252737482486653)
XLA Ops:
  0.6 100.5 %shard_map.85 = (bf16[8,256,128]{2,1,0:T(8,128)(2,1)}, bf16[3456,128]{1,0:T(8,128)(2,1)}, bf16[3456,128]{1,0:T(8,128)(2,1)}) custom-call(s32[16]{0:T(128)} %partner_ref.1, f32[16]{0:T(128)} %share_ref.1, bf16[8,256,128]{2,1,0:T(8,128)(2,1)} %bitcast.13, bf16[3,1152,128]{2,1,0:T(8,128)(2,1)} %bitcast.9, bf16[3,1152,128]{2,1,0:T(8,128)(2,1)} %bitcast.10, ...), custom_call_target="tpu_custom_call" | custom-call | tf_op jit(solution)/shard_map/pallas_call | solution.py:449
  101.2 0.0 copy-start
  101.2 2.7 %convert.2 = f32[3,3,3,128,128]{4,3,2,1,0:T(8,128)} convert(bf16[3,3,3,128,128]{4,3,2,1,0:T(8,128)(2,1)} %bitcast.12) | non-fusion elementwise | flops 442368 | bytes 2654208 | tf_op jit(solution)/shard_map/reshape | solution.py:507
  103.8 0.0 copy-done
  103.9 0.0 copy-start.1
  103.9 1.4 %convert.3 = f32[3,3,3,128,128]{4,3,2,1,0:T(8,128)} convert(bf16[3,3,3,128,128]{4,3,2,1,0:T(8,128)(2,1)S(1)} %bitcast.11) | non-fusion elementwise | flops 442368 | bytes 2654208 | tf_op jit(solution)/shard_map/reshape | solution.py:508
  105.3 0.0 copy-done.1
  105.3 0.8 copy.10
Async XLA Ops:
  101.2 2.7 %copy-start = (bf16[3456,128]{1,0:T(8,128)(2,1)S(1)}, bf16[3456,128]{1,0:T(8,128)(2,1)}, u32[]{:S(2)}) copy-start(bf16[3456,128]{1,0:T(8,128)(2,1)} %get-tuple-element.8) | copy-start | bytes 2654212
  103.9 1.4 %copy-start.1 = (bf16[8,256,128]{2,1,0:T(8,128)(2,1)S(1)}, bf16[8,256,128]{2,1,0:T(8,128)(2,1)}, u32[]{:S(2)}) copy-start(bf16[8,256,128]{2,1,0:T(8,128)(2,1)} %get-tuple-element.6) | copy-start | bytes 1572868

commit v5 on v4

--- a/solution.py
+++ b/solution.py
@@ -67,7 +67,12 @@
                 wide_ref[step, pl.ds(out * chans, chans), pl.ds(place * chans, chans)] = block
 
 
-def conv_pairs(store, wide_ref, first, spread, width, cells, back=False):
+def conv_pairs(store, wide_ref, pairs, spread, width, cells, back=False):
+    for at in range(0, len(pairs), 2):
+        yield from conv_chunk(store, wide_ref, pairs[at : at + 2], spread, width, cells, back)
+
+
+def conv_chunk(store, wide_ref, first, spread, width, cells, back):
     side = 1 if back else 0
     total = None
     for half in range(2):
@@ -95,7 +100,7 @@
 
 
 def grad_blocks(store, grad_at, depth, spread, width, cells):
-    ranges = ((0, 2 * spread, (0, 1)), (2 * spread, depth, (0, 1, 2)), (depth, depth + 2 * spread, (1, 2)))
+    ranges = ((2 * spread, depth, (0, 1, 2)), (0, 2 * spread, (0, 1)), (depth, depth + 2 * spread, (1, 2)))
     for low, high, depth_taps in ranges:
         lhs = jnp.concatenate(
             [taps(store, e, spread, width, cells) for e in range(low, high)], axis=0
@@ -406,9 +411,19 @@
     def grad_at(ref, p):
         return jnp.zeros((cells, chans), BF16) if p is None else ref[p]
 
-    total[...] = jnp.zeros_like(total)
-    for tap, part in grad_blocks(store_mix, functools.partial(grad_at, grad_ref), depth, 2, width, cells):
-        total[tap] += part
+    def gather(store, term, spread, fresh):
+        for place, (tap, part) in enumerate(
+            grad_blocks(store, functools.partial(grad_at, term), depth, spread, width, cells)
+        ):
+            if fresh and place < 3:
+                total[tap] = part
+            else:
+                total[tap] += part
+            if place == 2:
+                yield
+
+    for _ in gather(store_mix, grad_ref, 2, True):
+        pass
     hand_over(held_two)
     seconds = lanes(1, held_two, land_two, full_two)
     advance(seconds)
@@ -420,18 +435,19 @@
         term_own[p] = (value * slope_own_ref[p]).astype(BF16)
         term_mate[p] = (value * slope_mate_ref[p]).astype(BF16)
     advance(seconds)
-    total[...] = jnp.zeros_like(total)
-    for store, term in ((store_own, term_own), (store_mate, term_mate)):
-        for tap, part in grad_blocks(store, functools.partial(grad_at, term), depth, 1, width, cells):
-            total[tap] += part
+    for _ in gather(store_own, term_own, 1, True):
+        pass
+    advance(seconds)
+    for _ in gather(store_mate, term_mate, 1, False):
         advance(seconds)
+    advance(seconds)
     hand_over(held_one)
     firsts = lanes(0, held_one, land_one, full_one)
     for _ in range(2 * len(orders[0]) + 1):
         advance(firsts)
         advance(seconds)
-    out_one[...] = full_one[pl.ds(0, used)]
-    out_two[...] = full_two[pl.ds(0, used)]
+    out_one[...] = full_one[pl.ds(0, used)].astype(F32)
+    out_two[...] = full_two[pl.ds(0, used)].astype(F32)
 
 
 def whole_call(args, count, slabs, width):
@@ -445,7 +461,7 @@
     dma = pltpu.SemaphoreType.DMA
     slab = pltpu.VMEM((depth, cells, chans), BF16)
     wide_slab = pltpu.VMEM((depth, cells, chans), F32)
-    sums = jax.ShapeDtypeStruct((used, chans), BF16)
+    sums = jax.ShapeDtypeStruct((used, chans), F32)
     return pl.pallas_call(
         functools.partial(whole_body, count, slabs, width),
         out_shape=[jax.ShapeDtypeStruct((depth, cells, chans), BF16), sums, sums],
@@ -504,8 +520,8 @@
     shape = first_kernel.shape
     return (
         result.reshape(volume.shape),
-        first_sum.astype(F32).reshape(shape),
-        second_sum.astype(F32).reshape(shape),
+        first_sum.reshape(shape),
+        second_sum.reshape(shape),
     )
 
 

time: 106 us -> 105 us (level)
  local copies, waits for them, and re-layouts: 0.8 us -> 6.09 us
  other arithmetic: 4.07 us -> 0 us
  Pallas kernels: 101 us -> 98.2 us
    unnamed x5, local copies, waits for them, and re-layouts: 0.8 us -> 6.09 us
    reshape x2 -> x0, other arithmetic: 4.07 us -> none  [the longest x1 2.66 us: shards(): first_sum.astype(F32).reshape(shape)]
    pallas_call x1, Pallas kernels: 101 us -> 98.2 us  [whole_call(): pl.pallas_call(functools.partial(whole_body, count, slabs, width), out_sh...]
where the time goes in v5:
time: 105 us
  Pallas kernels  98.2 us (94%)
  local copies, waits for them, and re-layouts  6.09 us (6%)
    pallas_call x1, Pallas kernels, whole_call(): pl.pallas_call(functools.partial(whole_body, count, slabs, width), out_sh...  98.2 us
    unnamed x5, local copies, waits for them, and re-layouts  6.09 us

profile of v5, /device:TPU:0, one launch (start us, length us, event | category | flops | bytes accessed | tf_op | source)
XLA Modules:
  0.0 105.0 jit_solution(3204355095442591042)
XLA Ops:
  0.6 98.2 %shard_map.85 = (bf16[8,256,128]{2,1,0:T(8,128)(2,1)}, f32[3456,128]{1,0:T(8,128)}, f32[3456,128]{1,0:T(8,128)}) custom-call(s32[16]{0:T(128)} %partner_ref.1, f32[16]{0:T(128)} %share_ref.1, bf16[8,256,128]{2,1,0:T(8,128)(2,1)} %bitcast.11, bf16[3,1152,128]{2,1,0:T(8,128)(2,1)} %bitcast.9, bf16[3,1152,128]{2,1,0:T(8,128)(2,1)} %bitcast.10, ...), custom_call_target="tpu_custom_call" | custom-call | tf_op jit(solution)/shard_map/pallas_call | solution.py:465
  98.9 1.9 %copy.12 = bf16[1,8,16,16,128]{4,3,2,1,0:T(8,128)(2,1)} copy(bf16[1,8,16,16,128]{4,3,2,1,0:T(8,128)(2,1)} %bitcast.13) | data formatting | bytes 1048576
  100.8 0.0 copy-start
  100.8 3.0 %copy.13 = f32[3,3,3,128,128]{4,3,2,1,0:T(8,128)} copy(f32[3,3,3,128,128]{4,3,2,1,0:T(8,128)} %bitcast.8) | data formatting | bytes 3538944
  103.8 0.0 copy-done
  103.8 1.2 %copy.14 = f32[3,3,3,128,128]{4,3,2,1,0:T(8,128)} copy(f32[3,3,3,128,128]{4,3,2,1,0:T(8,128)S(1)} %bitcast.7) | data formatting | bytes 3538944
Async XLA Ops:
  100.8 3.0 %copy-start = (f32[3456,128]{1,0:T(8,128)S(1)}, f32[3456,128]{1,0:T(8,128)}, u32[]{:S(2)}) copy-start(f32[3456,128]{1,0:T(8,128)} %get-tuple-element.8) | copy-start | bytes 5308420

commit v6 on v5

--- a/solution.py
+++ b/solution.py
@@ -446,8 +446,8 @@
     for _ in range(2 * len(orders[0]) + 1):
         advance(firsts)
         advance(seconds)
-    out_one[...] = full_one[pl.ds(0, used)].astype(F32)
-    out_two[...] = full_two[pl.ds(0, used)].astype(F32)
+    out_one[...] = full_one[pl.ds(0, used)]
+    out_two[...] = full_two[pl.ds(0, used)]
 
 
 def whole_call(args, count, slabs, width):
@@ -461,7 +461,7 @@
     dma = pltpu.SemaphoreType.DMA
     slab = pltpu.VMEM((depth, cells, chans), BF16)
     wide_slab = pltpu.VMEM((depth, cells, chans), F32)
-    sums = jax.ShapeDtypeStruct((used, chans), F32)
+    sums = jax.ShapeDtypeStruct((used, chans), BF16)
     return pl.pallas_call(
         functools.partial(whole_body, count, slabs, width),
         out_shape=[jax.ShapeDtypeStruct((depth, cells, chans), BF16), sums, sums],
@@ -520,8 +520,8 @@
     shape = first_kernel.shape
     return (
         result.reshape(volume.shape),
-        first_sum.reshape(shape),
-        second_sum.reshape(shape),
+        first_sum.astype(F32).reshape(shape),
+        second_sum.astype(F32).reshape(shape),
     )
 
 

time: 105 us -> 103 us (0.981)
  local copies, waits for them, and re-layouts: 6.09 us -> 0.8 us
  other arithmetic: 0 us -> 4.07 us
    unnamed x5, local copies, waits for them, and re-layouts: 6.09 us -> 0.8 us
    reshape x0 -> x2, other arithmetic: none -> 4.07 us  [the longest x1 2.66 us: shards(): first_sum.astype(F32).reshape(shape)]
where the time goes in v6:
time: 103 us
  Pallas kernels  97.7 us (95%)
  other arithmetic  4.07 us (4%)
    pallas_call x1, Pallas kernels, whole_call(): pl.pallas_call(functools.partial(whole_body, count, slabs, width), out_sh...  97.7 us
    reshape x1, other arithmetic, shards(): first_sum.astype(F32).reshape(shape)  2.66 us

profile of v6, /device:TPU:0, one launch (start us, length us, event | category | flops | bytes accessed | tf_op | source)
XLA Modules:
  0.0 103.2 jit_solution(14960190710496140746)
XLA Ops:
  0.6 97.7 %shard_map.85 = (bf16[8,256,128]{2,1,0:T(8,128)(2,1)}, bf16[3456,128]{1,0:T(8,128)(2,1)}, bf16[3456,128]{1,0:T(8,128)(2,1)}) custom-call(s32[16]{0:T(128)} %partner_ref.1, f32[16]{0:T(128)} %share_ref.1, bf16[8,256,128]{2,1,0:T(8,128)(2,1)} %bitcast.13, bf16[3,1152,128]{2,1,0:T(8,128)(2,1)} %bitcast.9, bf16[3,1152,128]{2,1,0:T(8,128)(2,1)} %bitcast.10, ...), custom_call_target="tpu_custom_call" | custom-call | tf_op jit(solution)/shard_map/pallas_call | solution.py:465
  98.4 0.0 copy-start
  98.4 2.7 %convert.2 = f32[3,3,3,128,128]{4,3,2,1,0:T(8,128)} convert(bf16[3,3,3,128,128]{4,3,2,1,0:T(8,128)(2,1)} %bitcast.12) | non-fusion elementwise | flops 442368 | bytes 2654208 | tf_op jit(solution)/shard_map/reshape | solution.py:523
  101.0 0.0 copy-done
  101.0 0.0 copy-start.1
  101.0 1.4 %convert.3 = f32[3,3,3,128,128]{4,3,2,1,0:T(8,128)} convert(bf16[3,3,3,128,128]{4,3,2,1,0:T(8,128)(2,1)S(1)} %bitcast.11) | non-fusion elementwise | flops 442368 | bytes 2654208 | tf_op jit(solution)/shard_map/reshape | solution.py:524
  102.5 0.0 copy-done.1
  102.5 0.8 copy.10
Async XLA Ops:
  98.4 2.7 %copy-start = (bf16[3456,128]{1,0:T(8,128)(2,1)S(1)}, bf16[3456,128]{1,0:T(8,128)(2,1)}, u32[]{:S(2)}) copy-start(bf16[3456,128]{1,0:T(8,128)(2,1)} %get-tuple-element.8) | copy-start | bytes 2654212
  101.0 1.4 %copy-start.1 = (bf16[8,256,128]{2,1,0:T(8,128)(2,1)S(1)}, bf16[8,256,128]{2,1,0:T(8,128)(2,1)}, u32[]{:S(2)}) copy-start(bf16[8,256,128]{2,1,0:T(8,128)(2,1)} %get-tuple-element.6) | copy-start | bytes 1572868
